TPU v7x, 32 devices: a whole 2x2x4 slice. The times are simulated.
32 devices in a mesh: grp: 2 (over x), fsdp: 16 (over z, y, core).
Axes of the slice: x: 2, y: 2, z: 4, core: 2. Of those that a mesh axis runs over, the one named last changes fastest.
Arguments:
- latent: bfloat16 [512, 6144], P('grp'), parts along dimension 0, may hold values from -400 to 400
- adjoint: bfloat16 [512, 6144], P(('grp', 'fsdp')), parts along dimension 0, may hold values from -6 to 6
- shift_row: float32 [12288], P('grp'), parts along dimension 0, may hold values from -4 to 4
- scale_row: float32 [12288], P('grp'), parts along dimension 0, may hold values from -2.5 to 2.5
- gate_row: float32 [12288], P('grp'), parts along dimension 0, may hold values from -4 to 4
- b_up: bfloat16 [24576], P('fsdp'), may hold values from -3 to 3
- w_up: bfloat16 [6144, 24576], P(None, 'fsdp'), may hold values from -0.078125 to 0.078125
- w_down: bfloat16 [24576, 6144], P('fsdp'), may hold values from -0.0390625 to 0.0390625
Outputs:
- new_adjoint: float32 [512, 6144], P(('grp', 'fsdp')), parts along dimension 0
There are 2 independent parts, one for each index of `grp`. A program takes and returns all parts, laid end to end along the dimension named above; an argument that names none is the same for every part. Nothing has to cross between parts.
All inputs are finite; a program needn't handle non-finite values.
Results may differ from a plain program's by a relative error of at most 0.00064.
Values may be sent and summed in bfloat16 or wider, within the bound.
No kernel may reach another device: no remote copies, remote signals or barrier semaphores. Data moves between devices by JAX's collectives and lax.ppermute only.
A program may use at most 128 MiB of HBM per device.

v0:
```python
import jax
import jax.numpy as jnp
from jax import lax
from jax.sharding import PartitionSpec as P

step_scale = 0.5


def gelu_slope(u):
    k = 0.7978845608
    t = jnp.tanh(k * (u + 0.044715 * u * u * u))
    return 0.5 * (1.0 + t) + 0.5 * u * (1.0 - t * t) * k * (1.0 + 3.0 * 0.044715 * u * u)


def normalize(latent):
    values = latent.astype(jnp.float32)
    mean = jnp.mean(values, axis=1, keepdims=True)
    centred = values - mean
    rstd = lax.rsqrt(jnp.mean(centred * centred, axis=1, keepdims=True) + 1e-06)
    return (centred * rstd, rstd)


def per_device(latent, adjoint, shift_row, scale_row, gate_row, b_up, w_up, w_down):
    own_rows = adjoint.shape[0]
    start = lax.axis_index("fsdp") * own_rows
    normed, rstd = normalize(latent)
    hidden_in = (normed * (1.0 + scale_row) + shift_row).astype(jnp.bfloat16)
    all_adjoint = lax.all_gather(adjoint, "fsdp", axis=0, tiled=True)
    gated = (gate_row * all_adjoint.astype(jnp.float32)).astype(jnp.bfloat16)
    upper = jnp.dot(hidden_in, w_up, preferred_element_type=jnp.float32) + b_up.astype(jnp.float32)
    d_act = lax.dot_general(
        gated, w_down, (((1,), (1,)), ((), ())), preferred_element_type=jnp.float32
    )
    d_upper = (d_act * gelu_slope(upper)).astype(jnp.bfloat16)
    partial_sum = lax.dot_general(
        d_upper, w_up, (((1,), (1,)), ((), ())), preferred_element_type=jnp.float32
    )
    total = lax.psum(partial_sum, "fsdp")
    d_hidden = lax.dynamic_slice_in_dim(total, start, own_rows, 0)
    own_normed = lax.dynamic_slice_in_dim(normed, start, own_rows, 0)
    own_rstd = lax.dynamic_slice_in_dim(rstd, start, own_rows, 0)
    scaled = (1.0 + scale_row) * d_hidden
    first = jnp.mean(scaled, axis=1, keepdims=True)
    second = jnp.mean(scaled * own_normed, axis=1, keepdims=True)
    d_latent = own_rstd * (scaled - first - own_normed * second)
    return adjoint.astype(jnp.float32) + step_scale * d_latent


def solution(mesh):
    in_specs = (
        P("grp", None),
        P(("grp", "fsdp"), None),
        P("grp"),
        P("grp"),
        P("grp"),
        P("fsdp"),
        P(None, "fsdp"),
        P("fsdp", None),
    )
    out_specs = P(("grp", "fsdp"), None)
    return jax.shard_map(
        per_device, mesh=mesh, in_specs=in_specs, out_specs=out_specs, check_vma=False
    )
```

profile of v0, /device:TPU:0, one launch (start us, length us, event | category | flops | bytes accessed | tf_op | source)
XLA Modules:
  0.0 228.1 jit_solution(11235810555299476558)
XLA Ops:
  6.5 0.0 copy-start
  6.5 0.0 all-gather.2.cloned.1.call-start
  6.5 0.7 all-gather.2.cloned.1.call-update
  7.3 0.0 all-reduce.2.cloned.1.call-start
  7.3 0.9 convert_element_type.26
  8.2 0.0 copy-start.5
  8.2 0.0 copy-start.10
  8.2 2.4 %convert_reduce_fusion = f32[256]{0:T(256)S(1)} fusion(bf16[256,6144]{1,0:T(8,128)(2,1)} %param.8), kind=kLoop, calls=%fused_computation.1 | loop fusion | flops 3145472 | bytes 3146752 | tf_op jit(solution)/shard_map/reduce_sum | solution.py:17
  10.6 0.0 copy-done
  10.6 0.0 copy-start.6
  10.6 1.0 fusion.2
  11.6 0.0 copy-done.5
  11.6 0.0 copy-start.8
  11.6 0.0 copy-done.6
  11.6 0.6 copy-done.8
  12.2 0.0 copy-start.3
  12.2 0.6 copy-done.3
  12.8 0.0 copy-done.10
  12.8 0.0 copy-start.11
  12.8 10.3 %fusion.9 = f32[256,1536]{1,0:T(8,128)} fusion(bf16[6144,1536]{1,0:T(8,128)(2,1)} %param.14, f32[6144]{0:T(1024)S(1)} %copy-done.10, f32[6144]{0:T(1024)S(1)} %broadcast_add_fusion, f32[1536]{0:T(1024)S(1)} %convert_element_type.26, bf16[256,6144]{1,0:T(8,128)(2,1)S(1)} %copy-done, f32[256]{0:T(256)S(1)} %add_rsqrt_fusion, f32[256]{0:T(256)S(1)} %broadcast_multiply_fusion), kind=kOutput, calls=%fused_computation.13 | convolution fusion | flops 4841668608 | bytes 23650304 | tf_op jit(solution)/shard_map/dot_general | solution.py:30
  23.1 34.5 %all-gather.2.cloned.1.call-done = bf16[256,6144]{1,0:T(8,128)(2,1)} async-done(((bf16[16,6144]{1,0:T(8,128)(2,1)}), bf16[256,6144]{1,0:T(8,128)(2,1)}) %all-gather.2.cloned.1.call-update) | async-done | bytes 3145744 | tf_op jit(solution)/shard_map/all_gather | solution.py:28
  57.6 0.0 copy-done.11
  57.6 22.3 %fusion.16 = f32[256,6144]{1,0:T(8,128)} fusion(bf16[6144,1536]{1,0:T(8,128)(2,1)} %param.14, bf16[1536,6144]{1,0:T(8,128)(2,1)} %param.15, bf16[256,6144]{1,0:T(8,128)(2,1)} %all-gather.2.cloned.1.call-done, f32[6144]{0:T(1024)S(1)} %copy-done.11, f32[256,1536]{1,0:T(8,128)} %fusion.9), kind=kOutput, calls=%fused_computation.22 | convolution fusion | flops 9675866112 | bytes 48783360 | tf_op jit(solution)/shard_map/dot_general | solution.py:35
  79.9 0.0 copy-start.9
  79.9 0.0 copy-start.1
  79.9 0.0 copy-start.7
  79.9 0.0 all-reduce.2.cloned.1.call-update
  80.0 0.6 copy-done.9
  80.6 0.1 dynamic-slice.3
  80.7 1.2 copy-done.1
  81.8 0.0 copy-done.7
  81.8 0.0 copy-start.4
  81.8 0.0 copy-start.2
  81.8 4.0 %fusion = f32[256,6144]{1,0:T(8,128)} fusion(bf16[256,6144]{1,0:T(8,128)(2,1)S(1)} %copy-done.1, f32[256]{0:T(256)S(1)} %copy-done.9, f32[256]{0:T(256)S(1)} %copy-done.7), kind=kLoop, calls=%fused_computation.2 | loop fusion | flops 4718592 | bytes 9439232 | tf_op jit(solution)/shard_map/mul | solution.py:20
  85.8 132.1 %all-reduce.2.cloned.1.call-done = f32[256,6144]{1,0:T(8,128)} async-done(((f32[256,6144]{1,0:T(8,128)}), f32[256,6144]{1,0:T(8,128)}) %all-reduce.2.cloned.1.call-update) | async-done | bytes 6291472 | tf_op jit(solution)/shard_map/psum | solution.py:38
  217.9 0.0 copy-done.4
  217.9 1.3 fusion.24
  219.2 0.0 copy-done.2
  219.2 2.0 multiply_add_fusion.1
  (4 shorter events, 0.0 us)
Async XLA Ops:
  6.5 4.1 %copy-start = (bf16[256,6144]{1,0:T(8,128)(2,1)S(1)}, bf16[256,6144]{1,0:T(8,128)(2,1)}, u32[]{:S(2)}) copy-start(bf16[256,6144]{1,0:T(8,128)(2,1)} %param.8) | copy-start | bytes 9437188
  6.5 51.0 %all-gather.2.cloned.1.call-start = ((), (), s32[]{:S(2)}) async-start(), calls=%async_computation | async-start | bytes 3342336 | tf_op jit(solution)/shard_map/all_gather | solution.py:28
  7.3 210.6 %all-reduce.2.cloned.1.call-start = ((), (), s32[]{:S(2)}) async-start(), calls=%async_computation.1 | async-start | bytes 12582912 | tf_op jit(solution)/shard_map/psum | solution.py:38
  8.2 3.4 %copy-start.5 = (f32[6144]{0:T(1024)S(1)}, f32[6144]{0:T(1024)}, u32[]{:S(2)}) copy-start(f32[6144]{0:T(1024)} %param.11) | copy-start | bytes 73732
  8.2 4.6 %copy-start.10 = (f32[6144]{0:T(1024)S(1)}, f32[6144]{0:T(1024)}, u32[]{:S(2)}) copy-start(f32[6144]{0:T(1024)} %param.10) | copy-start | bytes 73732
  10.6 1.0 copy-start.6
  11.6 0.6 copy-start.8
  12.2 0.6 copy-start.3
  12.8 44.8 %copy-start.11 = (f32[6144]{0:T(1024)S(1)}, f32[6144]{0:T(1024)}, u32[]{:S(2)}) copy-start(f32[6144]{0:T(1024)} %param.12) | copy-start | bytes 73732
  79.9 0.7 copy-start.9
  79.9 1.9 copy-start.1
  79.9 1.9 copy-start.7
  81.8 136.1 %copy-start.4 = (f32[6144]{0:T(1024)S(1)}, f32[6144]{0:T(1024)}, u32[]{:S(2)}) copy-start(f32[6144]{0:T(1024)} %copy-done.3) | copy-start | bytes 73732
  81.8 137.4 %copy-start.2 = (bf16[16,6144]{1,0:T(8,128)(2,1)S(1)}, bf16[16,6144]{1,0:T(8,128)(2,1)}, u32[]{:S(2)}) copy-start(bf16[16,6144]{1,0:T(8,128)(2,1)} %param.9) | copy-start | bytes 589828
Sparse Core Ops, SparseCore 0:
  9.6 47.8 all-gather.1
  80.1 137.7 all-reduce.1
where the time goes:
time: 228 us
  waiting for transfers between devices  167 us (73%)
  matrix products  32.7 us (14%)
  between operations  13.5 us (6%)
  other arithmetic  11.6 us (5%)
  local copies, waits for them, and re-layouts  3.05 us (1%)
    psum x1, waiting for transfers between devices, per_device(): total = lax.psum(partial_sum, 'fsdp')  132 us
    all_gather x1, waiting for transfers between devices, per_device(): all_adjoint = lax.all_gather(adjoint, 'fsdp', axis=0, tiled=True)  34.5 us
    dot_general x1, matrix products, per_device(): lax.dot_general(d_upper, w_up, (((1,), (1,)), ((), ())), preferred_elemen...  22.3 us
    dot_general x1, matrix products, per_device(): jnp.dot(hidden_in, w_up, preferred_element_type=jnp.float32)  10.3 us
  transfers between devices with their start and end apart: 2, of which 2 were waited for; matrix products, arithmetic and copies ran while one was open for 8% of the time, Pallas kernels for 0%

commit v1 on v0

v1 whole, which is shorter than its diff:
```python
import jax
import jax.numpy as jnp
from jax import lax
from jax.sharding import PartitionSpec as P

step_scale = 0.5


def gelu_slope(u):
    k = 0.7978845608
    t = jnp.tanh(k * (u + 0.044715 * u * u * u))
    return 0.5 * (1.0 + t) + 0.5 * u * (1.0 - t * t) * k * (1.0 + 3.0 * 0.044715 * u * u)


def normalize(latent):
    values = latent.astype(jnp.float32)
    mean = jnp.mean(values, axis=1, keepdims=True)
    centred = values - mean
    rstd = lax.rsqrt(jnp.mean(centred * centred, axis=1, keepdims=True) + 1e-06)
    return (centred * rstd, rstd)


def finish(latent_rows, adjoint, scale_row, d_hidden):
    normed, rstd = normalize(latent_rows)
    scaled = (1.0 + scale_row) * d_hidden
    first = jnp.mean(scaled, axis=1, keepdims=True)
    second = jnp.mean(scaled * normed, axis=1, keepdims=True)
    d_latent = rstd * (scaled - first - normed * second)
    return adjoint.astype(jnp.float32) + step_scale * d_latent


def rows_t(a, b):
    return lax.dot_general(a, b, (((1,), (1,)), ((), ())), preferred_element_type=jnp.float32)


def general(latent, adjoint, shift_row, scale_row, gate_row, b_up, w_up, w_down):
    own_rows = adjoint.shape[0]
    start = lax.axis_index("fsdp") * own_rows
    normed, _ = normalize(latent)
    hidden_in = (normed * (1.0 + scale_row) + shift_row).astype(jnp.bfloat16)
    gated = (gate_row * adjoint.astype(jnp.float32)).astype(jnp.bfloat16)
    gated = lax.all_gather(gated, "fsdp", axis=0, tiled=True)
    upper = jnp.dot(hidden_in, w_up, preferred_element_type=jnp.float32) + b_up.astype(jnp.float32)
    d_upper = (rows_t(gated, w_down) * gelu_slope(upper)).astype(jnp.bfloat16)
    d_hidden = lax.psum_scatter(rows_t(d_upper, w_up), "fsdp", scatter_dimension=0, tiled=True)
    return finish(lax.dynamic_slice_in_dim(latent, start, own_rows, 0), adjoint, scale_row, d_hidden)


def middle(i):
    return (i >> 2) in (1, 2)


CORE = [(i, i ^ 1) for i in range(16)]
SIDE = [(i, i ^ 2) for i in range(16)]
SIDE_ENDS = [(i, i ^ 2) for i in range(16) if not middle(i)]
PAIR = [(i, i ^ 4) for i in range(16)]
PAIR_OUT = [(i, i ^ 4) for i in range(16) if middle(i)]
PAIR_IN = [(i, i ^ 4) for i in range(16) if not middle(i)]
MID = [(i, i ^ 12) for i in range(16) if middle(i)]


def send(x, pairs):
    return lax.ppermute(x, "fsdp", pairs)


def gather_rows(own, is_mid):
    b00 = own
    b01 = send(b00, SIDE)
    b10 = send(b00, PAIR)
    m1 = send(b00, MID)
    m2 = send(b10, MID)
    a2 = send(jnp.where(is_mid, m1, b01), PAIR)
    y2 = send(jnp.where(is_mid, m1, b10), SIDE)
    b20 = jnp.where(is_mid, m2, a2)
    b11 = jnp.where(is_mid, a2, y2)
    a3 = send(m2, PAIR_OUT)
    b21 = send(b20, SIDE)
    y4 = send(a3, SIDE_ENDS)
    b30 = jnp.where(is_mid, m1, a3)
    b31 = jnp.where(is_mid, y2, y4)
    return [b00, b01, b10, b11, b20, b21, b30, b31]


def scatter_sums(p, is_mid):
    half = lambda x: x.astype(jnp.float16)
    wide = lambda x: x.astype(jnp.float32)
    p00, p01, p10, p11, p20, p21, p30, p31 = p
    y4 = wide(send(half(p31), SIDE_ENDS))
    y3 = wide(send(half(p21), SIDE))
    a3 = wide(send(half(p30 + y4), PAIR_IN))
    y2 = wide(send(half(jnp.where(is_mid, p31, p11)), SIDE))
    p20 = p20 + y3 + a3
    a2 = wide(send(half(jnp.where(is_mid, p11, p20)), PAIR))
    m2 = wide(send(half(p20), MID))
    p10 = p10 + jnp.where(is_mid, m2, y2)
    p01 = p01 + jnp.where(is_mid, 0.0, a2)
    m1 = wide(send(half(p30 + y2 + a2), MID))
    a1 = wide(send(half(p10), PAIR))
    y1 = wide(send(half(p01), SIDE))
    return p00 + m1 + a1 + y1


def line_of_four(latent, adjoint, shift_row, scale_row, gate_row, b_up, w_up, w_down):
    rows = adjoint.shape[0]
    me = lax.axis_index("fsdp")
    z = me >> 2
    is_mid = (z == 1) | (z == 2)
    order = [dz * 4 + dy * 2 + dc for dc in range(2) for dz in range(4) for dy in range(2)]

    gated = (gate_row * adjoint.astype(jnp.float32)).astype(jnp.bfloat16)
    blocks = gather_rows(gated, is_mid)
    mine = jnp.concatenate(blocks, axis=0)
    gated = jnp.concatenate([mine, send(mine, CORE)], axis=0)

    normed, _ = normalize(latent)
    hidden_in = (normed * (1.0 + scale_row) + shift_row).astype(jnp.bfloat16)
    upper = jnp.dot(hidden_in, w_up, preferred_element_type=jnp.float32) + b_up.astype(jnp.float32)
    slope = gelu_slope(upper)
    slope = jnp.concatenate([lax.dynamic_slice_in_dim(slope, (me ^ k) * rows, rows, 0) for k in order], axis=0)

    unit = 16.0 * jnp.maximum(jnp.max(jnp.abs(gated.astype(jnp.float32)), axis=1, keepdims=True), 1e-30)
    d_upper = (rows_t(gated, w_down) * slope).astype(jnp.bfloat16)
    partial_sum = rows_t(d_upper, w_up) / unit
    n = 8 * rows
    partial_sum = partial_sum[:n] + send(partial_sum[n:].astype(jnp.float16), CORE).astype(jnp.float32)
    d_hidden = scatter_sums([partial_sum[k * rows : (k + 1) * rows] for k in range(8)], is_mid) * unit[:rows]
    return finish(lax.dynamic_slice_in_dim(latent, me * rows, rows, 0), adjoint, scale_row, d_hidden)


def solution(mesh):
    in_specs = (
        P("grp", None),
        P(("grp", "fsdp"), None),
        P("grp"),
        P("grp"),
        P("grp"),
        P("fsdp"),
        P(None, "fsdp"),
        P("fsdp", None),
    )
    out_specs = P(("grp", "fsdp"), None)
    body = line_of_four if mesh.shape["fsdp"] == 16 else general
    return jax.shard_map(body, mesh=mesh, in_specs=in_specs, out_specs=out_specs, check_vma=False)
```

time: 228 us -> 141 us (0.62)
  waiting for transfers between devices: 167 us -> 35.5 us
  starting transfers between devices: 0.04 us -> 28.5 us
  local copies, waits for them, and re-layouts: 3.05 us -> 23.4 us
  between operations: 13.5 us -> 0.24 us
  other arithmetic: 11.6 us -> 20.6 us
    psum x1 -> x0, waiting for transfers between devices: 132 us -> none  [per_device(): total = lax.psum(partial_sum, 'fsdp')]
    ppermute x0 -> x20, waiting for transfers between devices: none -> 35.5 us  [send(): return lax.ppermute(x, 'fsdp', pairs)]
    all_gather x1 -> x0, waiting for transfers between devices: 34.5 us -> none  [per_device(): all_adjoint = lax.all_gather(adjoint, 'fsdp', axis=0, tiled=True)]
    ppermute x0 -> x20, starting transfers between devices: none -> 28.5 us  [send(): return lax.ppermute(x, 'fsdp', pairs)]
    unnamed x24 -> x31, local copies, waits for them, and re-layouts: 2.97 us -> 21.4 us
    unnamed x0 -> x5, other arithmetic: none -> 5.84 us
    mul x1, other arithmetic: 4.01 us -> 0.01 us  [line_of_four(): 16.0 * jnp.maximum(jnp.max(jnp.abs(gated.astype(jnp.float32)), axis=1, ke...]
    add x2 -> x3, other arithmetic: 2.04 us -> 4.64 us  [the longest x1 2.35 us: line_of_four(): partial_sum[:n]]
  transfers between devices with their start and end apart: 2 -> 20, of which waited for: 2 -> 11; matrix products, arithmetic and copies ran while one was open for 8% -> 27% of each run, Pallas kernels for 0% -> 0%
where the time goes in v1:
time: 141 us; the launch traced here: 140 us
  waiting for transfers between devices  35.5 us (25%)
  matrix products  31.2 us (22%)
  starting transfers between devices  28.5 us (20%)
  local copies, waits for them, and re-layouts  23.4 us (17%)
  other arithmetic  20.6 us (15%)
    ppermute x20, waiting for transfers between devices, send(): return lax.ppermute(x, 'fsdp', pairs)  35.5 us
    ppermute x20, starting transfers between devices, send(): return lax.ppermute(x, 'fsdp', pairs)  28.5 us
    unnamed x31, local copies, waits for them, and re-layouts  21.4 us
    dot_general x1, matrix products, rows_t(): lax.dot_general(a, b, (((1,), (1,)), ((), ())), preferred_element_type=jn...  21 us
    dot_general x1, matrix products, line_of_four(): jnp.dot(hidden_in, w_up, preferred_element_type=jnp.float32)  10.3 us
    unnamed x5, other arithmetic  5.84 us
  transfers between devices with their start and end apart: 20, of which 11 were waited for; matrix products, arithmetic and copies ran while one was open for 27% of the time, Pallas kernels for 0%

profile of v1, /device:TPU:0, one launch (start us, length us, event | category | flops | bytes accessed | tf_op | source)
XLA Modules:
  0.0 139.5 jit_solution(232174678002266076)
XLA Ops:
  0.0 1.7 %constant_dynamic-update-slice_fusion.4 = (bf16[128,6144]{1,0:T(8,128)(2,1)}, bf16[16,6144]{1,0:T(8,128)(2,1)}) fusion(bf16[16,6144]{1,0:T(8,128)(2,1)} %param.9, f32[6144]{0:T(1024)} %param.12), kind=kLoop, calls=%fused_computation.95 | loop fusion | flops 294911 | bytes 614400
  1.7 3.0 %collective-permute-start = (bf16[16,6144]{1,0:T(8,128)(2,1)}, bf16[16,6144]{1,0:T(8,128)(2,1)S(1)}, u32[]{:S(2)}, u32[]{:S(2)}) collective-permute-start(bf16[16,6144]{1,0:T(8,128)(2,1)} %get-tuple-element.11), channel_id=1, source_target_pairs={{0,2},{1,3},{2,0},{3,1},{4,6},{5,7},{6,4},{7,5},{8,10},{9,11},{10,... | collective-permute-start | bytes 589832 | tf_op jit(solution)/shard_map/ppermute | solution.py:63
  4.7 1.6 %collective-permute-start.1 = (bf16[16,6144]{1,0:T(8,128)(2,1)}, bf16[16,6144]{1,0:T(8,128)(2,1)}, u32[]{:S(2)}, u32[]{:S(2)}) collective-permute-start(bf16[16,6144]{1,0:T(8,128)(2,1)} %get-tuple-element.11), channel_id=1, source_target_pairs={{0,4},{1,5},{2,6},{3,7},{4,0},{5,1},{6,2},{7,3},{8,12},{9,13},{10,... | collective-permute-start | bytes 589832 | tf_op jit(solution)/shard_map/ppermute | solution.py:63
  6.9 1.6 %constant_dynamic-update-slice_fusion.10 = bf16[256,6144]{1,0:T(8,128)(2,1)} fusion(bf16[16,6144]{1,0:T(8,128)(2,1)} %get-tuple-element.11), kind=kLoop, calls=%fused_computation.101 | loop fusion | bytes 393216
  8.6 1.3 broadcast_add_fusion
  9.9 2.5 %convert_reduce_fusion = f32[256]{0:T(256)S(1)} fusion(bf16[256,6144]{1,0:T(8,128)(2,1)} %param.8), kind=kLoop, calls=%fused_computation.1 | loop fusion | flops 3145472 | bytes 3146752 | tf_op jit(solution)/shard_map/reduce_sum | solution.py:17
  12.7 1.0 fusion.2
  13.7 10.3 %fusion.20 = f32[256,1536]{1,0:T(8,128)S(1)} fusion(bf16[6144,1536]{1,0:T(8,128)(2,1)} %param.14, bf16[256,6144]{1,0:T(8,128)(2,1)S(1)} %copy-done, f32[6144]{0:T(1024)} %param.10, f32[6144]{0:T(1024)} %broadcast_add_fusion, f32[256]{0:T(256)S(1)} %add_rsqrt_fusion, f32[256]{0:T(256)S(1)} %broadcast_multiply_fusion, f32[1536]{0:T(1024)S(1)} %convert_element_type.86), kind=kOutput, calls=%fused_computation.26 | convolution fusion | flops 4848353280 | bytes 23650304 | tf_op jit(solution)/shard_map/dot_general | solution.py:117
  24.0 1.2 copy-done.1
  25.8 1.5 %dynamic-slice_dynamic-update-slice_fusion.14 = f32[256,1536]{1,0:T(8,128)} fusion(f32[256,1536]{1,0:T(8,128)} %dynamic-slice_dynamic-update-slice_fusion.15, f32[256,1536]{1,0:T(8,128)} %copy-done.1, s32[]{:T(128)S(6)} %select_n.105), kind=kLoop, calls=%fused_computation.83 | loop fusion | bytes 196612
  27.4 1.5 %dynamic-slice_dynamic-update-slice_fusion.13 = f32[256,1536]{1,0:T(8,128)} fusion(f32[256,1536]{1,0:T(8,128)} %dynamic-slice_dynamic-update-slice_fusion.14, f32[256,1536]{1,0:T(8,128)} %copy-done.1, s32[]{:T(128)S(6)} %select_n.106), kind=kLoop, calls=%fused_computation.82 | loop fusion | bytes 196612
  28.9 1.5 %dynamic-slice_dynamic-update-slice_fusion.12 = f32[256,1536]{1,0:T(8,128)} fusion(f32[256,1536]{1,0:T(8,128)} %dynamic-slice_dynamic-update-slice_fusion.13, f32[256,1536]{1,0:T(8,128)} %copy-done.1, s32[]{:T(128)S(6)} %select_n.107), kind=kLoop, calls=%fused_computation.81 | loop fusion | bytes 196612
  30.4 1.5 %dynamic-slice_dynamic-update-slice_fusion.11 = f32[256,1536]{1,0:T(8,128)} fusion(f32[256,1536]{1,0:T(8,128)} %dynamic-slice_dynamic-update-slice_fusion.12, f32[256,1536]{1,0:T(8,128)} %copy-done.1, s32[]{:T(128)S(6)} %select_n.108), kind=kLoop, calls=%fused_computation.80 | loop fusion | bytes 196612
  32.0 1.5 %dynamic-slice_dynamic-update-slice_fusion.10 = f32[256,1536]{1,0:T(8,128)} fusion(f32[256,1536]{1,0:T(8,128)} %dynamic-slice_dynamic-update-slice_fusion.11, f32[256,1536]{1,0:T(8,128)} %copy-done.1, s32[]{:T(128)S(6)} %select_n.109), kind=kLoop, calls=%fused_computation.79 | loop fusion | bytes 196612
  33.5 1.5 %dynamic-slice_dynamic-update-slice_fusion.9 = f32[256,1536]{1,0:T(8,128)} fusion(f32[256,1536]{1,0:T(8,128)} %dynamic-slice_dynamic-update-slice_fusion.10, f32[256,1536]{1,0:T(8,128)} %copy-done.1, s32[]{:T(128)S(6)} %select_n.110), kind=kLoop, calls=%fused_computation.78 | loop fusion | bytes 196612
  35.0 1.7 %dynamic-slice_dynamic-update-slice_fusion.8 = f32[256,1536]{1,0:T(8,128)} fusion(f32[256,1536]{1,0:T(8,128)} %dynamic-slice_dynamic-update-slice_fusion.9, f32[256,1536]{1,0:T(8,128)} %copy-done.1, s32[]{:T(128)S(6)} %select_n.111), kind=kLoop, calls=%fused_computation.77 | loop fusion | bytes 196612
  36.7 0.8 constant_dynamic-update-slice_fusion.3
  37.5 1.8 %constant_dynamic-update-slice_fusion.2 = (bf16[128,6144]{1,0:T(8,128)(2,1)}, bf16[256,6144]{1,0:T(8,128)(2,1)}, bf16[16,6144]{1,0:T(8,128)(2,1)S(1)}, bf16[16,6144]{1,0:T(8,128)(2,1)S(1)}) fusion(bf16[128,6144]{1,0:T(8,128)(2,1)} %get-tuple-element.32, bf16[16,6144]{1,0:T(8,128)(2,1)} %collective-permute-done.1, bf16[256,6144]{1,0:T(8,128)(2,1)} %get-tuple-element.33, ...), kind=kLoop, calls=%fused_computation.93 | loop fusion | flops 196608 | bytes 1376257
  39.3 4.4 %collective-permute-start.3 = (bf16[16,6144]{1,0:T(8,128)(2,1)S(1)}, bf16[16,6144]{1,0:T(8,128)(2,1)S(1)}, u32[]{:S(2)}, u32[]{:S(2)}) collective-permute-start(bf16[16,6144]{1,0:T(8,128)(2,1)S(1)} %get-tuple-element.31), channel_id=1, source_target_pairs={{0,4},{1,5},{2,6},{3,7},{4,0},{5,1},{6,2},{7,3},{8,12},{9,13},{10,... | collective-permute-start | bytes 589832 | tf_op jit(solution)/shard_map/ppermute | solution.py:63
  45.5 2.2 %collective-permute-done.3 = bf16[16,6144]{1,0:T(8,128)(2,1)S(1)} collective-permute-done((bf16[16,6144]{1,0:T(8,128)(2,1)S(1)}, bf16[16,6144]{1,0:T(8,128)(2,1)S(1)}, u32[]{:S(2)}, u32[]{:S(2)}) %collective-permute-start.3) | collective-permute-done | bytes 196640 | tf_op jit(solution)/shard_map/ppermute | solution.py:63
  47.7 1.6 %collective-permute-done.4 = bf16[16,6144]{1,0:T(8,128)(2,1)S(1)} collective-permute-done((bf16[16,6144]{1,0:T(8,128)(2,1)S(1)}, bf16[16,6144]{1,0:T(8,128)(2,1)S(1)}, u32[]{:S(2)}, u32[]{:S(2)}) %collective-permute-start.4) | collective-permute-done | bytes 196640 | tf_op jit(solution)/shard_map/ppermute | solution.py:63
  49.3 0.8 fusion.45
  50.1 0.7 constant_dynamic-update-slice_fusion.1
  51.4 1.3 collective-permute-start.7
  52.7 0.7 constant_dynamic-update-slice_fusion.7
  53.4 6.4 %collective-permute-done.7 = bf16[16,6144]{1,0:T(8,128)(2,1)S(1)} collective-permute-done((bf16[16,6144]{1,0:T(8,128)(2,1)S(1)}, bf16[16,6144]{1,0:T(8,128)(2,1)S(1)}, u32[]{:S(2)}, u32[]{:S(2)}) %collective-permute-start.7) | collective-permute-done | bytes 196640 | tf_op jit(solution)/shard_map/ppermute | solution.py:63
  59.8 2.6 %collective-permute-start.8 = (bf16[16,6144]{1,0:T(8,128)(2,1)S(1)}, bf16[16,6144]{1,0:T(8,128)(2,1)S(1)}, u32[]{:S(2)}, u32[]{:S(2)}) collective-permute-start(bf16[16,6144]{1,0:T(8,128)(2,1)S(1)} %collective-permute-done.7), channel_id=1, source_target_pairs={{0,2},{1,3},{2,0},{3,1},{12,14},{13,15},{14,12},{15,13},{16,18},{1... | collective-permute-start | bytes 589832 | tf_op jit(solution)/shard_map/ppermute | solution.py:63
  62.4 0.8 constant_dynamic-update-slice_fusion
  63.2 0.8 fusion.47
  64.0 3.3 %collective-permute-done.8 = bf16[16,6144]{1,0:T(8,128)(2,1)S(1)} collective-permute-done((bf16[16,6144]{1,0:T(8,128)(2,1)S(1)}, bf16[16,6144]{1,0:T(8,128)(2,1)S(1)}, u32[]{:S(2)}, u32[]{:S(2)}) %collective-permute-start.8) | collective-permute-done | bytes 196640 | tf_op jit(solution)/shard_map/ppermute | solution.py:63
  67.3 0.8 fusion.49
  72.6 1.3 constant_dynamic-update-slice_fusion.5
  74.0 2.5 %abs_reduce_fusion = f32[256]{0:T(256)S(1)} fusion(bf16[256,6144]{1,0:T(8,128)(2,1)} %constant_dynamic-update-slice_fusion.5), kind=kLoop, calls=%fused_computation.9 | loop fusion | flops 4718336 | bytes 3146752 | tf_op jit(solution)/shard_map/reduce_max | solution.py:121
  76.5 21.0 %convolution_divide_fusion = f32[256,6144]{1,0:T(8,128)} fusion(bf16[6144,1536]{1,0:T(8,128)(2,1)} %param.14, f32[256]{0:T(256)S(1)} %maximum_multiply_fusion, f32[256,1536]{1,0:T(8,128)} %dynamic-slice_dynamic-update-slice_fusion, bf16[256,6144]{1,0:T(8,128)(2,1)} %constant_dynamic-update-slice_fusion.5, bf16[1536,6144]{1,0:T(8,128)(2,1)} %param.15), kind=kOutput, calls=%fused_computation.2 | convolution fusion | flops 9666035712 | bytes 48759808 | tf_op jit(solution)/shard_map/dot_general | solution.py:33
  97.5 2.1 %slice_convert_fusion = f16[128,6144]{1,0:T(8,128)(2,1)S(1)} fusion(f32[256,6144]{1,0:T(8,128)} %convolution_divide_fusion), kind=kLoop, calls=%fused_computation.11 | loop fusion | flops 786432 | bytes 4718592 | tf_op jit(solution)/shard_map/convert.1
  100.1 3.0 %collective-permute-done.10 = f16[128,6144]{1,0:T(8,128)(2,1)S(1)} collective-permute-done((f16[128,6144]{1,0:T(8,128)(2,1)S(1)}, f16[128,6144]{1,0:T(8,128)(2,1)S(1)}, u32[]{:S(2)}, u32[]{:S(2)}) %collective-permute-start.10) | collective-permute-done | bytes 1572896 | tf_op jit(solution)/shard_map/ppermute | solution.py:63
  103.2 2.3 %slice_add_fusion = f32[128,6144]{1,0:T(8,128)S(1)} fusion(f32[256,6144]{1,0:T(8,128)} %convolution_divide_fusion, f16[128,6144]{1,0:T(8,128)(2,1)S(1)} %collective-permute-done.10), kind=kLoop, calls=%fused_computation.12 | loop fusion | flops 1572864 | bytes 7864320 | tf_op jit(solution)/shard_map/add | solution.py:125
  105.6 2.6 %collective-permute-start.13 = (f16[16,6144]{1,0:T(8,128)(2,1)S(1)}, f16[16,6144]{1,0:T(8,128)(2,1)S(1)}, u32[]{:S(2)}, u32[]{:S(2)}) collective-permute-start(f16[16,6144]{1,0:T(8,128)(2,1)S(1)} %slice_convert_fusion.2), channel_id=1, source_target_pairs={{0,2},{1,3},{2,0},{3,1},{12,14},{13,15},{14,12},{15,13},{16,18},{1... | collective-permute-start | bytes 589832 | tf_op jit(solution)/shard_map/ppermute | solution.py:63
  108.2 6.4 %collective-permute-done.13 = f16[16,6144]{1,0:T(8,128)(2,1)S(1)} collective-permute-done((f16[16,6144]{1,0:T(8,128)(2,1)S(1)}, f16[16,6144]{1,0:T(8,128)(2,1)S(1)}, u32[]{:S(2)}, u32[]{:S(2)}) %collective-permute-start.13) | collective-permute-done | bytes 196640 | tf_op jit(solution)/shard_map/ppermute | solution.py:63
  114.7 1.3 collective-permute-start.14
  116.0 0.8 collective-permute-start.12
  116.9 3.2 %collective-permute-done.14 = f16[16,6144]{1,0:T(8,128)(2,1)S(1)} collective-permute-done((f16[16,6144]{1,0:T(8,128)(2,1)S(1)}, f16[16,6144]{1,0:T(8,128)(2,1)S(1)}, u32[]{:S(2)}, u32[]{:S(2)}) %collective-permute-start.14) | collective-permute-done | bytes 196640 | tf_op jit(solution)/shard_map/ppermute | solution.py:63
  120.1 2.3 %collective-permute-done.12 = f16[16,6144]{1,0:T(8,128)(2,1)S(1)} collective-permute-done((f16[16,6144]{1,0:T(8,128)(2,1)S(1)}, f16[16,6144]{1,0:T(8,128)(2,1)S(1)}, u32[]{:S(2)}, u32[]{:S(2)}) %collective-permute-start.12) | collective-permute-done | bytes 196640 | tf_op jit(solution)/shard_map/ppermute | solution.py:63
  124.5 3.8 %collective-permute-done.15 = f16[16,6144]{1,0:T(8,128)(2,1)S(1)} collective-permute-done((f16[16,6144]{1,0:T(8,128)(2,1)S(1)}, f16[16,6144]{1,0:T(8,128)(2,1)S(1)}, u32[]{:S(2)}, u32[]{:S(2)}) %collective-permute-start.15) | collective-permute-done | bytes 196640 | tf_op jit(solution)/shard_map/ppermute | solution.py:63
  128.8 0.8 collective-permute-start.19
  129.5 5.0 %collective-permute-start.18 = (f16[16,6144]{1,0:T(8,128)(2,1)S(1)}, f16[16,6144]{1,0:T(8,128)(2,1)S(1)}, u32[]{:S(2)}, u32[]{:S(2)}) collective-permute-start(f16[16,6144]{1,0:T(8,128)(2,1)S(1)} %get-tuple-element.15), channel_id=1, source_target_pairs={{0,4},{1,5},{2,6},{3,7},{4,0},{5,1},{6,2},{7,3},{8,12},{9,13},{10,... | collective-permute-start | bytes 589832 | tf_op jit(solution)/shard_map/ppermute | solution.py:63
  135.3 2.9 %collective-permute-done.18 = f16[16,6144]{1,0:T(8,128)(2,1)S(1)} collective-permute-done((f16[16,6144]{1,0:T(8,128)(2,1)S(1)}, f16[16,6144]{1,0:T(8,128)(2,1)S(1)}, u32[]{:S(2)}, u32[]{:S(2)}) %collective-permute-start.18) | collective-permute-done | bytes 196640 | tf_op jit(solution)/shard_map/ppermute | solution.py:63
  138.6 0.9 convert_add_fusion.2
  (55 shorter events, 12.8 us)
Async XLA Ops:
  1.7 35.0 %collective-permute-start = (bf16[16,6144]{1,0:T(8,128)(2,1)}, bf16[16,6144]{1,0:T(8,128)(2,1)S(1)}, u32[]{:S(2)}, u32[]{:S(2)}) collective-permute-start(bf16[16,6144]{1,0:T(8,128)(2,1)} %get-tuple-element.11), channel_id=1, source_target_pairs={{0,2},{1,3},{2,0},{3,1},{4,6},{5,7},{6,4},{7,5},{8,10},{9,11},{10,... | collective-permute-start | bytes 589832 | tf_op jit(solution)/shard_map/ppermute | solution.py:63
  4.7 32.8 %collective-permute-start.1 = (bf16[16,6144]{1,0:T(8,128)(2,1)}, bf16[16,6144]{1,0:T(8,128)(2,1)}, u32[]{:S(2)}, u32[]{:S(2)}) collective-permute-start(bf16[16,6144]{1,0:T(8,128)(2,1)} %get-tuple-element.11), channel_id=1, source_target_pairs={{0,4},{1,5},{2,6},{3,7},{4,0},{5,1},{6,2},{7,3},{8,12},{9,13},{10,... | collective-permute-start | bytes 589832 | tf_op jit(solution)/shard_map/ppermute | solution.py:63
  6.3 31.2 %collective-permute-start.2 = (bf16[16,6144]{1,0:T(8,128)(2,1)}, bf16[16,6144]{1,0:T(8,128)(2,1)S(1)}, u32[]{:S(2)}, u32[]{:S(2)}) collective-permute-start(bf16[16,6144]{1,0:T(8,128)(2,1)} %get-tuple-element.11), channel_id=1, source_target_pairs={{4,8},{5,9},{6,10},{7,11},{8,4},{9,5},{10,6},{11,7},{20,24},{21,25... | collective-permute-start | bytes 589832 | tf_op jit(solution)/shard_map/ppermute | solution.py:63
  9.9 2.8 %copy-start = (bf16[256,6144]{1,0:T(8,128)(2,1)S(1)}, bf16[256,6144]{1,0:T(8,128)(2,1)}, u32[]{:S(2)}) copy-start(bf16[256,6144]{1,0:T(8,128)(2,1)} %param.8) | copy-start | bytes 9437188
  12.7 1.0 copy-start.5
  24.0 1.2 copy-start.1
  35.0 9.1 %copy-start.2 = (f32[256,1536]{1,0:T(8,128)S(1)}, f32[256,1536]{1,0:T(8,128)}, u32[]{:S(2)}) copy-start(f32[256,1536]{1,0:T(8,128)} %copy-done.1) | copy-start | bytes 4718596
  39.3 8.5 %collective-permute-start.3 = (bf16[16,6144]{1,0:T(8,128)(2,1)S(1)}, bf16[16,6144]{1,0:T(8,128)(2,1)S(1)}, u32[]{:S(2)}, u32[]{:S(2)}) collective-permute-start(bf16[16,6144]{1,0:T(8,128)(2,1)S(1)} %get-tuple-element.31), channel_id=1, source_target_pairs={{0,4},{1,5},{2,6},{3,7},{4,0},{5,1},{6,2},{7,3},{8,12},{9,13},{10,... | collective-permute-start | bytes 589832 | tf_op jit(solution)/shard_map/ppermute | solution.py:63
  43.6 5.7 %collective-permute-start.4 = (bf16[16,6144]{1,0:T(8,128)(2,1)S(1)}, bf16[16,6144]{1,0:T(8,128)(2,1)S(1)}, u32[]{:S(2)}, u32[]{:S(2)}) collective-permute-start(bf16[16,6144]{1,0:T(8,128)(2,1)S(1)} %get-tuple-element.30), channel_id=1, source_target_pairs={{0,2},{1,3},{2,0},{3,1},{4,6},{5,7},{6,4},{7,5},{8,10},{9,11},{10,... | collective-permute-start | bytes 589832 | tf_op jit(solution)/shard_map/ppermute | solution.py:63
  44.8 5.3 %collective-permute-start.5 = (bf16[16,6144]{1,0:T(8,128)(2,1)}, bf16[16,6144]{1,0:T(8,128)(2,1)S(1)}, u32[]{:S(2)}, u32[]{:S(2)}) collective-permute-start(bf16[16,6144]{1,0:T(8,128)(2,1)} %collective-permute-done.1), channel_id=1, source_target_pairs={{4,8},{5,9},{6,10},{7,11},{8,4},{9,5},{10,6},{11,7},{20,24},{21,25... | collective-permute-start | bytes 589832 | tf_op jit(solution)/shard_map/ppermute | solution.py:63
  50.9 11.5 %collective-permute-start.6 = (bf16[16,6144]{1,0:T(8,128)(2,1)S(1)}, bf16[16,6144]{1,0:T(8,128)(2,1)S(1)}, u32[]{:S(2)}, u32[]{:S(2)}) collective-permute-start(bf16[16,6144]{1,0:T(8,128)(2,1)S(1)} %get-tuple-element.9), channel_id=1, source_target_pairs={{0,2},{1,3},{2,0},{3,1},{4,6},{5,7},{6,4},{7,5},{8,10},{9,11},{10,... | collective-permute-start | bytes 589832 | tf_op jit(solution)/shard_map/ppermute | solution.py:63
  51.4 8.4 %collective-permute-start.7 = (bf16[16,6144]{1,0:T(8,128)(2,1)S(1)}, bf16[16,6144]{1,0:T(8,128)(2,1)S(1)}, u32[]{:S(2)}, u32[]{:S(2)}) collective-permute-start(bf16[16,6144]{1,0:T(8,128)(2,1)S(1)} %collective-permute-done.5), channel_id=1, source_target_pairs={{4,0},{5,1},{6,2},{7,3},{8,12},{9,13},{10,14},{11,15},{20,16},{21,... | collective-permute-start | bytes 589832 | tf_op jit(solution)/shard_map/ppermute | solution.py:63
  59.8 7.6 %collective-permute-start.8 = (bf16[16,6144]{1,0:T(8,128)(2,1)S(1)}, bf16[16,6144]{1,0:T(8,128)(2,1)S(1)}, u32[]{:S(2)}, u32[]{:S(2)}) collective-permute-start(bf16[16,6144]{1,0:T(8,128)(2,1)S(1)} %collective-permute-done.7), channel_id=1, source_target_pairs={{0,2},{1,3},{2,0},{3,1},{12,14},{13,15},{14,12},{15,13},{16,18},{1... | collective-permute-start | bytes 589832 | tf_op jit(solution)/shard_map/ppermute | solution.py:63
  68.1 4.5 %collective-permute-start.9 = (bf16[128,6144]{1,0:T(8,128)(2,1)}, bf16[128,6144]{1,0:T(8,128)(2,1)S(1)}, u32[]{:S(2)}, u32[]{:S(2)}) collective-permute-start(bf16[128,6144]{1,0:T(8,128)(2,1)} %get-tuple-element.20), channel_id=1, source_target_pairs={{0,1},{1,0},{2,3},{3,2},{4,5},{5,4},{6,7},{7,6},{8,9},{9,8},{10,11... | collective-permute-start | bytes 4718600 | tf_op jit(solution)/shard_map/ppermute | solution.py:63
  99.6 3.6 %collective-permute-start.10 = (f16[128,6144]{1,0:T(8,128)(2,1)S(1)}, f16[128,6144]{1,0:T(8,128)(2,1)S(1)}, u32[]{:S(2)}, u32[]{:S(2)}) collective-permute-start(f16[128,6144]{1,0:T(8,128)(2,1)S(1)} %slice_convert_fusion), channel_id=1, source_target_pairs={{0,1},{1,0},{2,3},{3,2},{4,5},{5,4},{6,7},{7,6},{8,9},{9,8},{10,11... | collective-permute-start | bytes 4718600 | tf_op jit(solution)/shard_map/ppermute | solution.py:63
  105.6 9.1 %collective-permute-start.13 = (f16[16,6144]{1,0:T(8,128)(2,1)S(1)}, f16[16,6144]{1,0:T(8,128)(2,1)S(1)}, u32[]{:S(2)}, u32[]{:S(2)}) collective-permute-start(f16[16,6144]{1,0:T(8,128)(2,1)S(1)} %slice_convert_fusion.2), channel_id=1, source_target_pairs={{0,2},{1,3},{2,0},{3,1},{12,14},{13,15},{14,12},{15,13},{16,18},{1... | collective-permute-start | bytes 589832 | tf_op jit(solution)/shard_map/ppermute | solution.py:63
  114.7 5.4 %collective-permute-start.14 = (f16[16,6144]{1,0:T(8,128)(2,1)S(1)}, f16[16,6144]{1,0:T(8,128)(2,1)S(1)}, u32[]{:S(2)}, u32[]{:S(2)}) collective-permute-start(f16[16,6144]{1,0:T(8,128)(2,1)S(1)} %get-tuple-element.19), channel_id=1, source_target_pairs={{0,4},{1,5},{2,6},{3,7},{12,8},{13,9},{14,10},{15,11},{16,20},{17,... | collective-permute-start | bytes 589832 | tf_op jit(solution)/shard_map/ppermute | solution.py:63
  116.0 6.4 %collective-permute-start.12 = (f16[16,6144]{1,0:T(8,128)(2,1)S(1)}, f16[16,6144]{1,0:T(8,128)(2,1)S(1)}, u32[]{:S(2)}, u32[]{:S(2)}) collective-permute-start(f16[16,6144]{1,0:T(8,128)(2,1)S(1)} %get-tuple-element.18), channel_id=1, source_target_pairs={{0,2},{1,3},{2,0},{3,1},{4,6},{5,7},{6,4},{7,5},{8,10},{9,11},{10,... | collective-permute-start | bytes 589832 | tf_op jit(solution)/shard_map/ppermute | solution.py:63
  122.6 15.6 %copy-start.4 = (f32[6144]{0:T(1024)S(1)}, f32[6144]{0:T(1024)}, u32[]{:S(2)}) copy-start(f32[6144]{0:T(1024)} %broadcast_add_fusion) | copy-start | bytes 73732
  122.6 5.7 %collective-permute-start.15 = (f16[16,6144]{1,0:T(8,128)(2,1)S(1)}, f16[16,6144]{1,0:T(8,128)(2,1)S(1)}, u32[]{:S(2)}, u32[]{:S(2)}) collective-permute-start(f16[16,6144]{1,0:T(8,128)(2,1)S(1)} %get-tuple-element.13), channel_id=1, source_target_pairs={{0,4},{1,5},{2,6},{3,7},{4,0},{5,1},{6,2},{7,3},{8,12},{9,13},{10,... | collective-permute-start | bytes 589832 | tf_op jit(solution)/shard_map/ppermute | solution.py:63
  122.9 5.7 %collective-permute-start.11 = (f16[16,6144]{1,0:T(8,128)(2,1)S(1)}, f16[16,6144]{1,0:T(8,128)(2,1)S(1)}, u32[]{:S(2)}, u32[]{:S(2)}) collective-permute-start(f16[16,6144]{1,0:T(8,128)(2,1)S(1)} %get-tuple-element.17), channel_id=1, source_target_pairs={{0,2},{1,3},{2,0},{3,1},{4,6},{5,7},{6,4},{7,5},{8,10},{9,11},{10,... | collective-permute-start | bytes 589832 | tf_op jit(solution)/shard_map/ppermute | solution.py:63
  123.6 5.0 %collective-permute-start.17 = (f16[16,6144]{1,0:T(8,128)(2,1)S(1)}, f16[16,6144]{1,0:T(8,128)(2,1)S(1)}, u32[]{:S(2)}, u32[]{:S(2)}) collective-permute-start(f16[16,6144]{1,0:T(8,128)(2,1)S(1)} %get-tuple-element.12), channel_id=1, source_target_pairs={{4,8},{5,9},{6,10},{7,11},{8,4},{9,5},{10,6},{11,7},{20,24},{21,25... | collective-permute-start | bytes 589832 | tf_op jit(solution)/shard_map/ppermute | solution.py:63
  124.5 14.1 %copy-start.3 = (bf16[16,6144]{1,0:T(8,128)(2,1)S(1)}, bf16[16,6144]{1,0:T(8,128)(2,1)}, u32[]{:S(2)}) copy-start(bf16[16,6144]{1,0:T(8,128)(2,1)} %param.9) | copy-start | bytes 589828
  128.8 6.5 %collective-permute-start.19 = (f16[16,6144]{1,0:T(8,128)(2,1)S(1)}, f16[16,6144]{1,0:T(8,128)(2,1)S(1)}, u32[]{:S(2)}, u32[]{:S(2)}) collective-permute-start(f16[16,6144]{1,0:T(8,128)(2,1)S(1)} %get-tuple-element.16), channel_id=1, source_target_pairs={{0,2},{1,3},{2,0},{3,1},{4,6},{5,7},{6,4},{7,5},{8,10},{9,11},{10,... | collective-permute-start | bytes 589832 | tf_op jit(solution)/shard_map/ppermute | solution.py:63
  129.5 8.7 %collective-permute-start.18 = (f16[16,6144]{1,0:T(8,128)(2,1)S(1)}, f16[16,6144]{1,0:T(8,128)(2,1)S(1)}, u32[]{:S(2)}, u32[]{:S(2)}) collective-permute-start(f16[16,6144]{1,0:T(8,128)(2,1)S(1)} %get-tuple-element.15), channel_id=1, source_target_pairs={{0,4},{1,5},{2,6},{3,7},{4,0},{5,1},{6,2},{7,3},{8,12},{9,13},{10,... | collective-permute-start | bytes 589832 | tf_op jit(solution)/shard_map/ppermute | solution.py:63
  134.6 3.6 %collective-permute-start.16 = (f16[16,6144]{1,0:T(8,128)(2,1)S(1)}, f16[16,6144]{1,0:T(8,128)(2,1)S(1)}, u32[]{:S(2)}, u32[]{:S(2)}) collective-permute-start(f16[16,6144]{1,0:T(8,128)(2,1)S(1)} %get-tuple-element.14), channel_id=1, source_target_pairs={{4,8},{5,9},{6,10},{7,11},{8,4},{9,5},{10,6},{11,7},{20,24},{21,25... | collective-permute-start | bytes 589832 | tf_op jit(solution)/shard_map/ppermute | solution.py:63

commit v2 on v0

v2 whole, which is shorter than its diff:
```python
import functools
import jax
import jax.numpy as jnp
from jax import lax
from jax.experimental import pallas as pl
from jax.experimental.pallas import tpu as pltpu
from jax.sharding import PartitionSpec as P

step_scale = 0.5


def gelu_slope(u):
    k = 0.7978845608
    t = jnp.tanh(k * (u + 0.044715 * u * u * u))
    return 0.5 * (1.0 + t) + 0.5 * u * (1.0 - t * t) * k * (1.0 + 3.0 * 0.044715 * u * u)


def normalize(latent):
    values = latent.astype(jnp.float32)
    mean = jnp.mean(values, axis=1, keepdims=True)
    centred = values - mean
    rstd = lax.rsqrt(jnp.mean(centred * centred, axis=1, keepdims=True) + 1e-06)
    return (centred * rstd, rstd)


def finish(latent_rows, adjoint, scale_row, d_hidden):
    normed, rstd = normalize(latent_rows)
    scaled = (1.0 + scale_row) * d_hidden
    first = jnp.mean(scaled, axis=1, keepdims=True)
    second = jnp.mean(scaled * normed, axis=1, keepdims=True)
    d_latent = rstd * (scaled - first - normed * second)
    return adjoint.astype(jnp.float32) + step_scale * d_latent


def rows_t(a, b):
    return lax.dot_general(a, b, (((1,), (1,)), ((), ())), preferred_element_type=jnp.float32)


def general(latent, adjoint, shift_row, scale_row, gate_row, b_up, w_up, w_down):
    own_rows = adjoint.shape[0]
    start = lax.axis_index("fsdp") * own_rows
    normed, _ = normalize(latent)
    hidden_in = (normed * (1.0 + scale_row) + shift_row).astype(jnp.bfloat16)
    gated = (gate_row * adjoint.astype(jnp.float32)).astype(jnp.bfloat16)
    gated = lax.all_gather(gated, "fsdp", axis=0, tiled=True)
    upper = jnp.dot(hidden_in, w_up, preferred_element_type=jnp.float32) + b_up.astype(jnp.float32)
    d_upper = (rows_t(gated, w_down) * gelu_slope(upper)).astype(jnp.bfloat16)
    d_hidden = lax.psum_scatter(rows_t(d_upper, w_up), "fsdp", scatter_dimension=0, tiled=True)
    return finish(lax.dynamic_slice_in_dim(latent, start, own_rows, 0), adjoint, scale_row, d_hidden)


def middle(i):
    return (i >> 2) in (1, 2)


CORE = [(i, i ^ 1) for i in range(16)]
SIDE = [(i, i ^ 2) for i in range(16)]
PAIR = [(i, i ^ 4) for i in range(16)]
CROSS = [(i, i ^ 12) for i in range(16)]
CROSS_MID = [(i, i ^ 12) for i in range(16) if middle(i)]


def send(x, pairs):
    return lax.ppermute(x, "fsdp", pairs)


def half(x):
    return x.astype(jnp.float16)


def wide(x):
    return x.astype(jnp.float32)


def after(x, *done):
    return lax.optimization_barrier((x, *done))[0]


def scatter_sums(quarters, is_mid, rows):
    near_early, near_late, far_early, far_late = quarters
    late = near_late + wide(send(half(far_late), CORE))
    p30, p31, p20, p21 = [late[k * rows : (k + 1) * rows] for k in range(4)]
    y2 = send(half(p21), SIDE)
    early = near_early + wide(send(half(far_early), CORE))
    p00, p01, p10, p11 = [early[k * rows : (k + 1) * rows] for k in range(4)]
    p20 = p20 + wide(y2)
    a2 = send(half(p20), PAIR)
    m2 = send(half(p20), CROSS_MID)
    y3 = send(after(half(p31), y2), SIDE)
    y1 = send(after(half(p11), y3), SIDE)
    p30 = p30 + wide(y3) + jnp.where(is_mid, wide(a2), 0.0)
    x = send(half(p30), CROSS)
    y0 = send(after(half(p01), y1), SIDE)
    a1 = send(half(p10 + wide(y1) + wide(m2)), PAIR)
    return p00 + wide(y0) + wide(x) + wide(a1)


VMEM = pl.BlockSpec(memory_space=pltpu.VMEM)
SMEM = pl.BlockSpec(memory_space=pltpu.SMEM)
HBM = pl.BlockSpec(memory_space=pltpu.HBM)


def kernel(body, specs, out_shape, flops, moved, grant, **more):
    several = isinstance(out_shape, (list, tuple))
    return pl.pallas_call(
        body,
        in_specs=specs,
        out_specs=[VMEM] * len(out_shape) if several else VMEM,
        out_shape=out_shape,
        compiler_params=pltpu.CompilerParams(vmem_limit_bytes=grant * 2**20),
        cost_estimate=pl.CostEstimate(flops=flops, bytes_accessed=moved, transcendentals=0),
        **more,
    )


def load(source, target, sem):
    copy = pltpu.make_async_copy(source, target, sem)
    copy.start()
    return copy


def load_parts(source, start, buf, sems):
    n = buf.shape[1]
    return [load(source.at[pl.ds(start + k * n, n)], buf.at[k], sems.at[k]) for k in range(buf.shape[0])]


def normalize_rows(rows, me_ref, latent_ref, shift_ref, scale_ref, h_ref, own_ref, rstd_ref):
    def block(p):
        g = (p >> 1) & 3
        owner = me_ref[0] ^ ((p >> 3) | ((p & 1) << 1) | ((g ^ (g >> 1)) << 2))
        values = latent_ref[pl.ds(pl.multiple_of(owner * rows, rows), rows), :].astype(jnp.float32)
        mean = jnp.mean(values, axis=1, keepdims=True)
        centred = values - mean
        rstd = lax.rsqrt(jnp.mean(centred * centred, axis=1, keepdims=True) + 1e-06)
        normed = centred * rstd
        h = normed * (1.0 + scale_ref[...]) + shift_ref[...]
        h_ref[pl.ds(pl.multiple_of(p * rows, rows), rows), :] = h.astype(h_ref.dtype)
        return normed, rstd

    own_ref[...], rstd_ref[...] = block(0)

    def step(p, _):
        block(p)
        return 0

    lax.fori_loop(1, 16, step, 0, unroll=3)


def add_products(acc, start, h_ref, copies, w_buf):
    n = w_buf.shape[1]
    for k, copy in enumerate(copies):
        copy.wait()
        product = jnp.dot(h_ref[:, start + k * n : start + (k + 1) * n], w_buf[k], preferred_element_type=jnp.float32)
        acc = product if acc is None else acc + product
    return acc


def first_kernel(rows, me_ref, latent_ref, shift_ref, scale_ref, wu_ref, wd_ref, h_ref, own_ref, rstd_ref, u_ref, wd_out, latent_buf, shift_buf, scale_buf, w_buf, sems, w_sems, wd_sem):
    copies = [
        load(source, target, sems.at[k])
        for k, (source, target) in enumerate([(latent_ref, latent_buf), (shift_ref, shift_buf), (scale_ref, scale_buf)])
    ]
    w_copies = load_parts(wu_ref, 0, w_buf, w_sems)
    wd_copy = load(wd_ref.at[pl.ds(0, wd_out.shape[0])], wd_out, wd_sem)
    for copy in copies:
        copy.wait()
    normalize_rows(rows, me_ref, latent_buf, shift_buf, scale_buf, h_ref, own_ref, rstd_ref)
    u_ref[...] = add_products(None, 0, h_ref, w_copies, w_buf)
    wd_copy.wait()


def second_kernel(start, h_ref, u_ref, wu_ref, u_out, w_buf, w_sems):
    u_out[...] = add_products(u_ref[...], start, h_ref, load_parts(wu_ref, start, w_buf, w_sems), w_buf)


def third_kernel(start, h_ref, u_ref, b_ref, wu_ref, slope_out, w_buf, w_sems):
    second_kernel(start, h_ref, u_ref, wu_ref, slope_out, w_buf, w_sems)
    width = slope_out.shape[1] // 3
    for j in range(3):
        cut = slice(j * width, (j + 1) * width)
        slope_out[:, cut] = gelu_slope(slope_out[:, cut] + b_ref[:, cut].astype(jnp.float32))


def du_kernel(*refs):
    pieces, (wd_early, slope_ref, wd_ref, wu_ref), (du_ref, unit_ref, wu_out, wd_buf, sems) = refs[:6], refs[6:10], refs[10:]
    early, late = wd_early.shape[0], wd_buf.shape[0]
    wd_copy = load(wd_ref.at[pl.ds(early, late)], wd_buf, sems.at[0])
    wu_copy = load(wu_ref.at[pl.ds(0, wu_out.shape[0])], wu_out, sems.at[1])
    at = 0
    for piece in pieces:
        top = jnp.max(jnp.abs(piece[...].astype(jnp.float32)), axis=1, keepdims=True)
        unit_ref[at : at + piece.shape[0], :] = 16.0 * jnp.maximum(top, 1e-30)
        at += piece.shape[0]
    gated = jnp.concatenate([piece[...] for piece in pieces], axis=0)
    for at in range(0, early + late, late):
        if at == early:
            wd_copy.wait()
        wd = wd_early[at : at + late, :] if at < early else wd_buf[...]
        du_ref[:, at : at + late] = (rows_t(gated, wd) * slope_ref[:, at : at + late]).astype(du_ref.dtype)
    wu_copy.wait()


def dh_kernel(du_ref, unit_ref, early_ref, wu_ref, *refs):
    outs, (w_buf, sems) = refs[:-2], refs[-2:]
    n, early, width = outs[0].shape[0], early_ref.shape[0], w_buf.shape[1]
    copies = load_parts(wu_ref, early, w_buf, sems)
    scale = 1.0 / unit_ref[...]
    for at in range(0, wu_ref.shape[0], width):
        if at < early:
            w = early_ref[at : at + width, :]
        else:
            k = (at - early) // width
            copies[k].wait()
            w = w_buf[k]
        dh = rows_t(du_ref[...], w) * scale
        for j, out in enumerate(outs):
            out[:, at : at + width] = dh[j * n : (j + 1) * n]


def finish_kernel(sum_ref, unit_ref, own_ref, rstd_ref, scale_ref, adjoint_ref, out_ref):
    normed = own_ref[...]
    scaled = (1.0 + scale_ref[...]) * (sum_ref[...] * unit_ref[: normed.shape[0], :])
    first = jnp.mean(scaled, axis=1, keepdims=True)
    second = jnp.mean(scaled * normed, axis=1, keepdims=True)
    d_latent = rstd_ref[...] * (scaled - first - normed * second)
    out_ref[...] = adjoint_ref[...].astype(jnp.float32) + step_scale * d_latent


def line_of_four(latent, adjoint, shift_row, scale_row, gate_row, b_up, w_up, w_down):
    rows, d = adjoint.shape
    tokens, ff = latent.shape[0], w_up.shape[1]
    me = lax.axis_index("fsdp")
    z = me >> 2
    is_mid = (z == 1) | (z == 2)
    f32, bf16 = jnp.float32, jnp.bfloat16
    work = 2 * tokens * d * ff
    shape = jax.ShapeDtypeStruct
    stay = lambda x: pltpu.with_memory_space_constraint(x, pltpu.HBM)
    w_up, w_down = stay(w_up), stay(w_down)
    scale = scale_row[None]

    b00 = (gate_row * adjoint.astype(f32)).astype(bf16)
    b30 = send(b00, CROSS)
    b10 = send(b00, PAIR)
    b01 = send(b00, SIDE)

    third, depth = ff // 3, d // 6
    u_shape = shape((tokens, ff), f32)
    w_scratch = [pltpu.VMEM((2, depth, ff), bf16)]
    w_sems = [pltpu.SemaphoreType.DMA((2,))]
    h, own_normed, own_rstd, u, wd_early = kernel(
        functools.partial(first_kernel, rows),
        [SMEM] + [HBM] * 5,
        [shape((tokens, d), bf16), shape((rows, d), f32), shape((rows, 1), f32), u_shape, shape((2 * third, d), bf16)],
        work // 2, 4 * d * third, 18,
        scratch_shapes=[pltpu.VMEM((tokens, d), bf16), pltpu.VMEM((1, d), f32), pltpu.VMEM((1, d), f32)]
        + w_scratch + [pltpu.SemaphoreType.DMA((3,))] + w_sems + [pltpu.SemaphoreType.DMA],
    )(me.reshape(1).astype(jnp.int32), stay(latent), stay(shift_row[None]), stay(scale), w_up, w_down)

    b10, b30 = after(b10, u), after(b30, u)
    m2 = send(b10, CROSS_MID)
    a2 = send(b30, PAIR)
    b11 = send(b10, SIDE)
    b31 = send(b30, SIDE)
    u = kernel(
        functools.partial(second_kernel, 2 * depth),
        [VMEM] * 2 + [HBM],
        u_shape,
        work // 3, 2 * d * third, 12,
        scratch_shapes=w_scratch + w_sems,
    )(h, after(u, b10, b30), w_up)

    b20 = after(jnp.where(is_mid, m2, a2), u)
    b21 = send(b20, SIDE)
    slope = kernel(
        functools.partial(third_kernel, 4 * depth),
        [VMEM] * 3 + [HBM],
        u_shape,
        work // 3, 2 * d * third, 12,
        scratch_shapes=w_scratch + w_sems,
    )(h, after(u, b20), b_up[None], w_up)

    cat = lambda *blocks: jnp.concatenate(blocks, axis=0)
    pieces = [cat(b00, b01, b10, b11), cat(b30, b31), cat(b20, b21)]
    pieces = pieces + [send(x, CORE) for x in pieces]
    early = 2 * depth
    du, unit, wu_early = kernel(
        du_kernel,
        [VMEM] * 8 + [HBM] * 2,
        [shape((tokens, ff), bf16), shape((tokens, 1), f32), shape((early, ff), bf16)],
        work, 2 * d * ff, 16,
        scratch_shapes=[pltpu.VMEM((third, d), bf16), pltpu.SemaphoreType.DMA((2,))],
    )(*pieces, wd_early, slope, w_down, w_up)
    quarters = kernel(
        dh_kernel,
        [VMEM] * 3 + [HBM],
        [shape((tokens // 4, d), f32)] * 4,
        work, 2 * d * ff, 20,
        scratch_shapes=[pltpu.VMEM((4, depth, ff), bf16), pltpu.SemaphoreType.DMA((4,))],
    )(du, unit, wu_early, w_up)
    return kernel(
        finish_kernel,
        [VMEM] * 6,
        shape((rows, d), f32),
        20 * rows * d, 10 * rows * d, 8,
    )(scatter_sums(quarters, is_mid, rows), unit, own_normed, own_rstd, scale, adjoint)


def solution(mesh):
    in_specs = (
        P("grp", None),
        P(("grp", "fsdp"), None),
        P("grp"),
        P("grp"),
        P("grp"),
        P("fsdp"),
        P(None, "fsdp"),
        P("fsdp", None),
    )
    out_specs = P(("grp", "fsdp"), None)
    body = line_of_four if mesh.shape["fsdp"] == 16 else general
    return jax.shard_map(body, mesh=mesh, in_specs=in_specs, out_specs=out_specs, check_vma=False)
```

time: 228 us -> 80.7 us (0.35)
  waiting for transfers between devices: 167 us -> 23.6 us
  matrix products: 32.7 us -> 0 us
  Pallas kernels: 0 us -> 29.3 us
  starting transfers between devices: 0.04 us -> 25.2 us
  between operations: 13.5 us -> 0.27 us
  other arithmetic: 11.6 us -> 2.02 us
  local copies, waits for them, and re-layouts: 3.05 us -> 0.21 us
    psum x1 -> x0, waiting for transfers between devices: 132 us -> none  [per_device(): total = lax.psum(partial_sum, 'fsdp')]
    all_gather x1 -> x0, waiting for transfers between devices: 34.5 us -> none  [per_device(): all_adjoint = lax.all_gather(adjoint, 'fsdp', axis=0, tiled=True)]
    dot_general x2 -> x0, matrix products: 32.7 us -> none  [the longest x1 22.3 us: per_device(): lax.dot_general(d_upper, w_up, (((1,), (1,)), ((), ())), preferred_elemen...]
    pallas_call x0 -> x6, Pallas kernels: none -> 29.3 us  [the longest x1 8.05 us: line_of_four(): kernel(functools.partial(first_kernel, rows), [SMEM] + [HBM] * 5, [shape(...]
    ppermute x0 -> x21, starting transfers between devices: none -> 25.2 us  [send(): return lax.ppermute(x, 'fsdp', pairs)]
    ppermute x0 -> x21, waiting for transfers between devices: none -> 23.6 us  [send(): return lax.ppermute(x, 'fsdp', pairs)]
    reduce_sum x3 -> x0, other arithmetic: 4.66 us -> none  [the longest x1 2.41 us: normalize(): mean = jnp.mean(values, axis=1, keepdims=True)]
    mul x1 -> x0, other arithmetic: 4.01 us -> none  [normalize(): return (centred * rstd, rstd)]
  transfers between devices with their start and end apart: 2 -> 21, of which waited for: 2 -> 9; matrix products, arithmetic and copies ran while one was open for 8% -> 1% of each run, Pallas kernels for 0% -> 21%
where the time goes in v2:
time: 80.7 us; the launch traced here: 80.6 us
  Pallas kernels  29.3 us (36%)
  starting transfers between devices  25.2 us (31%)
  waiting for transfers between devices  23.6 us (29%)
  other arithmetic  2.02 us (3%)
    ppermute x21, starting transfers between devices, send(): return lax.ppermute(x, 'fsdp', pairs)  25.2 us
    ppermute x21, waiting for transfers between devices, send(): return lax.ppermute(x, 'fsdp', pairs)  23.6 us
    pallas_call x1, Pallas kernels, line_of_four(): kernel(functools.partial(first_kernel, rows), [SMEM] + [HBM] * 5, [shape(...  8.05 us
    pallas_call x1, Pallas kernels, line_of_four(): kernel(dh_kernel, [VMEM] * 3 + [HBM], [shape((tokens // 4, d), f32)] * 4,...  6.19 us
    pallas_call x1, Pallas kernels, line_of_four(): kernel(du_kernel, [VMEM] * 8 + [HBM] * 2, [shape((tokens, ff), bf16), sha...  5.46 us
    pallas_call x1, Pallas kernels, line_of_four(): kernel(functools.partial(third_kernel, 4 * depth), [VMEM] * 3 + [HBM], u_...  4.64 us
    pallas_call x1, Pallas kernels, line_of_four(): kernel(functools.partial(second_kernel, 2 * depth), [VMEM] * 2 + [HBM], u...  3.85 us
  transfers between devices with their start and end apart: 21, of which 9 were waited for; matrix products, arithmetic and copies ran while one was open for 1% of the time, Pallas kernels for 21%

profile of v2, /device:TPU:0, one launch (start us, length us, event | category | flops | bytes accessed | tf_op | source)
XLA Modules:
  0.0 80.6 jit_solution(1681043952546101803)
XLA Ops:
  0.0 1.0 %multiply_convert_fusion = bf16[16,6144]{1,0:T(8,128)(2,1)S(1)} fusion(bf16[16,6144]{1,0:T(8,128)(2,1)} %adjoint_ref.1, f32[6144]{0:T(1024)} %param.12), kind=kLoop, calls=%fused_computation.14 | loop fusion | flops 294912 | bytes 417792 | tf_op jit(solution)/shard_map/convert_element_type | solution.py:242
  1.0 5.1 %collective-permute-start.3 = (bf16[16,6144]{1,0:T(8,128)(2,1)S(1)}, bf16[16,6144]{1,0:T(8,128)(2,1)S(1)}, u32[]{:S(2)}, u32[]{:S(2)}) collective-permute-start(bf16[16,6144]{1,0:T(8,128)(2,1)S(1)} %multiply_convert_fusion), channel_id=1, source_target_pairs={{0,12},{1,13},{2,14},{3,15},{4,8},{5,9},{6,10},{7,11},{8,4},{9,5},... | collective-permute-start | bytes 589832 | tf_op jit(solution)/shard_map/ppermute | solution.py:64
  6.1 1.5 %collective-permute-start = (bf16[16,6144]{1,0:T(8,128)(2,1)S(1)}, bf16[16,6144]{1,0:T(8,128)(2,1)S(1)}, u32[]{:S(2)}, u32[]{:S(2)}) collective-permute-start(bf16[16,6144]{1,0:T(8,128)(2,1)S(1)} %multiply_convert_fusion), channel_id=1, source_target_pairs={{0,2},{1,3},{2,0},{3,1},{4,6},{5,7},{6,4},{7,5},{8,10},{9,11},{10,... | collective-permute-start | bytes 589832 | tf_op jit(solution)/shard_map/ppermute | solution.py:64
  7.6 8.0 %shard_map.82 = (bf16[256,6144]{1,0:T(8,128)(2,1)S(1)}, f32[16,6144]{1,0:T(8,128)S(1)}, f32[16,1]{1,0:T(8,128)S(1)}, f32[256,1536]{1,0:T(8,128)S(1)}, bf16[1024,6144]{1,0:T(8,128)(2,1)S(1)}) custom-call(s32[1]{0:T(128)} %bitcast.me_ref, bf16[256,6144]{1,0:T(8,128)(2,1)} %latent_ref.1, f32[1,6144]{1,0:T(1,128)} %bitcast.5, f32[1,6144]{1,0:T(1,128)} %bitcast.3, ...), custom_call_target="tpu_custom_call" | custom-call | flops 2415919104 | bytes 12582912 | tf_op jit(solution)/shard_map/pallas_call | solution.py:251
  15.7 0.9 %collective-permute-start.5 = (bf16[16,6144]{1,0:T(8,128)(2,1)S(1)}, bf16[16,6144]{1,0:T(8,128)(2,1)S(1)}, u32[]{:S(2)}, u32[]{:S(2)}) collective-permute-start(bf16[16,6144]{1,0:T(8,128)(2,1)S(1)} %collective-permute-done.1), channel_id=1, source_target_pairs={{4,8},{5,9},{6,10},{7,11},{8,4},{9,5},{10,6},{11,7},{20,24},{21,25... | collective-permute-start | bytes 589832 | tf_op jit(solution)/shard_map/ppermute | solution.py:64
  16.5 1.2 %collective-permute-start.2 = (bf16[16,6144]{1,0:T(8,128)(2,1)S(1)}, bf16[16,6144]{1,0:T(8,128)(2,1)S(1)}, u32[]{:S(2)}, u32[]{:S(2)}) collective-permute-start(bf16[16,6144]{1,0:T(8,128)(2,1)S(1)} %collective-permute-done.1), channel_id=1, source_target_pairs={{0,2},{1,3},{2,0},{3,1},{4,6},{5,7},{6,4},{7,5},{8,10},{9,11},{10,... | collective-permute-start | bytes 589832 | tf_op jit(solution)/shard_map/ppermute | solution.py:64
  17.7 2.9 %collective-permute-start.6 = (bf16[16,6144]{1,0:T(8,128)(2,1)S(1)}, bf16[16,6144]{1,0:T(8,128)(2,1)S(1)}, u32[]{:S(2)}, u32[]{:S(2)}) collective-permute-start(bf16[16,6144]{1,0:T(8,128)(2,1)S(1)} %collective-permute-done.3), channel_id=1, source_target_pairs={{0,4},{1,5},{2,6},{3,7},{4,0},{5,1},{6,2},{7,3},{8,12},{9,13},{10,... | collective-permute-start | bytes 589832 | tf_op jit(solution)/shard_map/ppermute | solution.py:64
  20.7 1.2 %collective-permute-start.4 = (bf16[16,6144]{1,0:T(8,128)(2,1)S(1)}, bf16[16,6144]{1,0:T(8,128)(2,1)S(1)}, u32[]{:S(2)}, u32[]{:S(2)}) collective-permute-start(bf16[16,6144]{1,0:T(8,128)(2,1)S(1)} %collective-permute-done.3), channel_id=1, source_target_pairs={{0,2},{1,3},{2,0},{3,1},{4,6},{5,7},{6,4},{7,5},{8,10},{9,11},{10,... | collective-permute-start | bytes 589832 | tf_op jit(solution)/shard_map/ppermute | solution.py:64
  21.9 3.9 %shard_map.83.u_ref = f32[256,1536]{1,0:T(8,128)S(1)} custom-call(bf16[256,6144]{1,0:T(8,128)(2,1)S(1)} %get-tuple-element.28.h_ref, f32[256,1536]{1,0:T(8,128)S(1)} %get-tuple-element.29.u_ref, bf16[6144,1536]{1,0:T(8,128)(2,1)} %wu_ref.7), custom_call_target="tpu_custom_call" | custom-call | flops 1610612736 | bytes 6291456 | tf_op jit(solution)/shard_map/pallas_call | solution.py:265
  25.8 0.0 copy-start.2
  25.8 0.9 %collective-permute-start.7 = (bf16[16,6144]{1,0:T(8,128)(2,1)S(1)}, bf16[16,6144]{1,0:T(8,128)(2,1)S(1)}, u32[]{:S(2)}, u32[]{:S(2)}) collective-permute-start(bf16[16,6144]{1,0:T(8,128)(2,1)S(1)} %broadcast_select_fusion), channel_id=1, source_target_pairs={{0,2},{1,3},{2,0},{3,1},{4,6},{5,7},{6,4},{7,5},{8,10},{9,11},{10,... | collective-permute-start | bytes 589832 | tf_op jit(solution)/shard_map/ppermute | solution.py:64
  26.7 1.0 %collective-permute-done.4 = bf16[16,6144]{1,0:T(8,128)(2,1)S(1)} collective-permute-done((bf16[16,6144]{1,0:T(8,128)(2,1)S(1)}, bf16[16,6144]{1,0:T(8,128)(2,1)S(1)}, u32[]{:S(2)}, u32[]{:S(2)}) %collective-permute-start.4) | collective-permute-done | bytes 196640 | tf_op jit(solution)/shard_map/ppermute | solution.py:64
  27.8 0.1 collective-permute-start.9
  27.9 0.1 pad_maximum_fusion.refs_0_
  27.9 0.5 collective-permute-start.8
  28.5 3.1 %collective-permute-done.7 = bf16[16,6144]{1,0:T(8,128)(2,1)S(1)} collective-permute-done((bf16[16,6144]{1,0:T(8,128)(2,1)S(1)}, bf16[16,6144]{1,0:T(8,128)(2,1)S(1)}, u32[]{:S(2)}, u32[]{:S(2)}) %collective-permute-start.7) | collective-permute-done | bytes 196640 | tf_op jit(solution)/shard_map/ppermute | solution.py:64
  31.6 0.1 collective-permute-start.10
  31.7 4.6 %shard_map.84.refs_7_ = f32[256,1536]{1,0:T(8,128)S(1)} custom-call(bf16[256,6144]{1,0:T(8,128)(2,1)S(1)} %get-tuple-element.28.h_ref, f32[256,1536]{1,0:T(8,128)S(1)} %shard_map.83.u_ref, bf16[1,1536]{1,0:T(2,128)(2,1)S(1)} %broadcast_in_dim.16.b_ref, bf16[6144,1536]{1,0:T(8,128)(2,1)} %wu_ref.7), custom_call_target="tpu_custom_call" | custom-call | flops 1610612736 | bytes 6291456 | tf_op jit(solution)/shard_map/pallas_call | solution.py:275
  36.4 5.5 %shard_map.85 = (bf16[256,1536]{1,0:T(8,128)(2,1)S(1)}, f32[256,1]{1,0:T(8,128)S(1)}, bf16[2048,1536]{1,0:T(8,128)(2,1)S(1)}) custom-call(bf16[64,6144]{1,0:T(8,128)(2,1)S(1)} %pad_maximum_fusion.refs_0_, bf16[32,6144]{1,0:T(8,128)(2,1)S(1)} %constant_dynamic-update-slice_fusion.refs_1_, bf16[32,6144]{1,0:T(8,128)(2,1)S(1)} %constant_dynamic-update-slice_fusion.2.refs_2_, ...), custom_call_target="tpu_custom_call" | custom-call | flops 4831838208 | bytes 18874368 | tf_op jit(solution)/shard_map/pallas_call | solution.py:287
  41.8 6.2 %shard_map.86 = (f32[64,6144]{1,0:T(8,128)S(1)}, f32[64,6144]{1,0:T(8,128)S(1)}, f32[64,6144]{1,0:T(8,128)S(1)}, f32[64,6144]{1,0:T(8,128)S(1)}) custom-call(bf16[256,1536]{1,0:T(8,128)(2,1)S(1)} %get-tuple-element.33.du_ref, f32[256,1]{1,0:T(8,128)S(1)} %get-tuple-element.34.unit_ref, bf16[2048,1536]{1,0:T(8,128)(2,1)S(1)} %get-tuple-element.35.early_ref, ...), custom_call_target="tpu_custom_call" | custom-call | flops 4831838208 | bytes 18874368 | tf_op jit(solution)/shard_map/pallas_call | solution.py:294
  48.0 0.1 convert_element_type.60
  48.1 0.5 collective-permute-start.12
  48.7 0.1 convert_element_type.58
  48.8 0.1 collective-permute-start.11
  48.9 1.7 %collective-permute-done.12 = f16[64,6144]{1,0:T(8,128)(2,1)S(1)} collective-permute-done((f16[64,6144]{1,0:T(8,128)(2,1)S(1)}, f16[64,6144]{1,0:T(8,128)(2,1)S(1)}, u32[]{:S(2)}, u32[]{:S(2)}) %collective-permute-start.12) | collective-permute-done | bytes 786464 | tf_op jit(solution)/shard_map/ppermute | solution.py:64
  50.6 0.2 fusion.8
  50.8 0.1 fusion.10
  50.9 1.5 %collective-permute-start.13 = (f16[16,6144]{1,0:T(8,128)(2,1)S(1)}, f16[16,6144]{1,0:T(8,128)(2,1)S(1)}, u32[]{:S(2)}, u32[]{:S(2)}) collective-permute-start(f16[16,6144]{1,0:T(8,128)(2,1)S(1)} %get-tuple-element.52), channel_id=1, source_target_pairs={{0,2},{1,3},{2,0},{3,1},{4,6},{5,7},{6,4},{7,5},{8,10},{9,11},{10,... | collective-permute-start | bytes 589832 | tf_op jit(solution)/shard_map/ppermute | solution.py:64
  52.4 0.2 fusion.7
  52.6 5.5 %collective-permute-done.13 = f16[16,6144]{1,0:T(8,128)(2,1)S(1)} collective-permute-done((f16[16,6144]{1,0:T(8,128)(2,1)S(1)}, f16[16,6144]{1,0:T(8,128)(2,1)S(1)}, u32[]{:S(2)}, u32[]{:S(2)}) %collective-permute-start.13) | collective-permute-done | bytes 196640 | tf_op jit(solution)/shard_map/ppermute | solution.py:64
  58.1 0.1 fusion.2
  58.2 2.6 %collective-permute-start.17 = (f16[16,6144]{1,0:T(8,128)(2,1)S(1)}, f16[16,6144]{1,0:T(8,128)(2,1)S(1)}, u32[]{:S(2)}, u32[]{:S(2)}) collective-permute-start(f16[16,6144]{1,0:T(8,128)(2,1)S(1)} %fusion.2), channel_id=1, source_target_pairs={{0,4},{1,5},{2,6},{3,7},{4,0},{5,1},{6,2},{7,3},{8,12},{9,13},{10,... | collective-permute-start | bytes 589832 | tf_op jit(solution)/shard_map/ppermute | solution.py:64
  60.8 0.8 collective-permute-start.14
  61.6 0.1 fusion.9
  61.7 0.7 collective-permute-start.19
  62.3 4.5 %collective-permute-done.14 = f16[16,6144]{1,0:T(8,128)(2,1)S(1)} collective-permute-done((f16[16,6144]{1,0:T(8,128)(2,1)S(1)}, f16[16,6144]{1,0:T(8,128)(2,1)S(1)}, u32[]{:S(2)}, u32[]{:S(2)}) %collective-permute-start.14) | collective-permute-done | bytes 196640 | tf_op jit(solution)/shard_map/ppermute | solution.py:64
  66.9 0.8 collective-permute-start.15
  67.7 0.1 fusion.4
  67.8 2.7 %collective-permute-start.18 = (f16[16,6144]{1,0:T(8,128)(2,1)S(1)}, f16[16,6144]{1,0:T(8,128)(2,1)S(1)}, u32[]{:S(2)}, u32[]{:S(2)}) collective-permute-start(f16[16,6144]{1,0:T(8,128)(2,1)S(1)} %fusion.4), channel_id=1, source_target_pairs={{0,12},{1,13},{2,14},{3,15},{4,8},{5,9},{6,10},{7,11},{8,4},{9,5},... | collective-permute-start | bytes 589832 | tf_op jit(solution)/shard_map/ppermute | solution.py:64
  70.5 2.2 %collective-permute-done.15 = f16[16,6144]{1,0:T(8,128)(2,1)S(1)} collective-permute-done((f16[16,6144]{1,0:T(8,128)(2,1)S(1)}, f16[16,6144]{1,0:T(8,128)(2,1)S(1)}, u32[]{:S(2)}, u32[]{:S(2)}) %collective-permute-start.15) | collective-permute-done | bytes 196640 | tf_op jit(solution)/shard_map/ppermute | solution.py:64
  72.7 0.8 collective-permute-start.16
  73.5 0.1 fusion.1
  73.6 0.3 collective-permute-start.20
  73.9 2.2 %collective-permute-done.18 = f16[16,6144]{1,0:T(8,128)(2,1)S(1)} collective-permute-done((f16[16,6144]{1,0:T(8,128)(2,1)S(1)}, f16[16,6144]{1,0:T(8,128)(2,1)S(1)}, u32[]{:S(2)}, u32[]{:S(2)}) %collective-permute-start.18) | collective-permute-done | bytes 196640 | tf_op jit(solution)/shard_map/ppermute | solution.py:64
  76.1 2.3 %collective-permute-done.16 = f16[16,6144]{1,0:T(8,128)(2,1)S(1)} collective-permute-done((f16[16,6144]{1,0:T(8,128)(2,1)S(1)}, f16[16,6144]{1,0:T(8,128)(2,1)S(1)}, u32[]{:S(2)}, u32[]{:S(2)}) %collective-permute-start.16) | collective-permute-done | bytes 196640 | tf_op jit(solution)/shard_map/ppermute | solution.py:64
  78.3 1.0 %collective-permute-done.20 = f16[16,6144]{1,0:T(8,128)(2,1)S(1)} collective-permute-done((f16[16,6144]{1,0:T(8,128)(2,1)S(1)}, f16[16,6144]{1,0:T(8,128)(2,1)S(1)}, u32[]{:S(2)}, u32[]{:S(2)}) %collective-permute-start.20) | collective-permute-done | bytes 196640 | tf_op jit(solution)/shard_map/ppermute | solution.py:64
  79.3 0.1 fusion.6.sum_ref
  79.5 1.1 %shard_map.87 = f32[16,6144]{1,0:T(8,128)} custom-call(f32[16,6144]{1,0:T(8,128)S(1)} %fusion.6.sum_ref, f32[256,1]{1,0:T(8,128)S(1)} %get-tuple-element.34.unit_ref, f32[16,6144]{1,0:T(8,128)S(1)} %get-tuple-element.43.own_ref, f32[16,1]{1,0:T(8,128)S(1)} %get-tuple-element.44.rstd_ref, f32[1,6144]{1,0:T(1,128)S(1)} %bitcast.4, bf16[16,6144]{1,0:T(8,128)(2,1)S(1)} %copy-done), custom_call_target="tpu_custom_call" | custom-call | flops 1966080 | bytes 983040 | tf_op jit(solution)/shard_map/pallas_call | solution.py:301
  (24 shorter events, 0.1 us)
Async XLA Ops:
  1.0 16.8 %collective-permute-start.3 = (bf16[16,6144]{1,0:T(8,128)(2,1)S(1)}, bf16[16,6144]{1,0:T(8,128)(2,1)S(1)}, u32[]{:S(2)}, u32[]{:S(2)}) collective-permute-start(bf16[16,6144]{1,0:T(8,128)(2,1)S(1)} %multiply_convert_fusion), channel_id=1, source_target_pairs={{0,12},{1,13},{2,14},{3,15},{4,8},{5,9},{6,10},{7,11},{8,4},{9,5},... | collective-permute-start | bytes 589832 | tf_op jit(solution)/shard_map/ppermute | solution.py:64
  6.1 9.6 %collective-permute-start.1 = (bf16[16,6144]{1,0:T(8,128)(2,1)S(1)}, bf16[16,6144]{1,0:T(8,128)(2,1)S(1)}, u32[]{:S(2)}, u32[]{:S(2)}) collective-permute-start(bf16[16,6144]{1,0:T(8,128)(2,1)S(1)} %multiply_convert_fusion), channel_id=1, source_target_pairs={{0,4},{1,5},{2,6},{3,7},{4,0},{5,1},{6,2},{7,3},{8,12},{9,13},{10,... | collective-permute-start | bytes 589832 | tf_op jit(solution)/shard_map/ppermute | solution.py:64
  6.1 21.8 %collective-permute-start = (bf16[16,6144]{1,0:T(8,128)(2,1)S(1)}, bf16[16,6144]{1,0:T(8,128)(2,1)S(1)}, u32[]{:S(2)}, u32[]{:S(2)}) collective-permute-start(bf16[16,6144]{1,0:T(8,128)(2,1)S(1)} %multiply_convert_fusion), channel_id=1, source_target_pairs={{0,2},{1,3},{2,0},{3,1},{4,6},{5,7},{6,4},{7,5},{8,10},{9,11},{10,... | collective-permute-start | bytes 589832 | tf_op jit(solution)/shard_map/ppermute | solution.py:64
  15.7 10.1 %collective-permute-start.5 = (bf16[16,6144]{1,0:T(8,128)(2,1)S(1)}, bf16[16,6144]{1,0:T(8,128)(2,1)S(1)}, u32[]{:S(2)}, u32[]{:S(2)}) collective-permute-start(bf16[16,6144]{1,0:T(8,128)(2,1)S(1)} %collective-permute-done.1), channel_id=1, source_target_pairs={{4,8},{5,9},{6,10},{7,11},{8,4},{9,5},{10,6},{11,7},{20,24},{21,25... | collective-permute-start | bytes 589832 | tf_op jit(solution)/shard_map/ppermute | solution.py:64
  16.5 11.3 %collective-permute-start.2 = (bf16[16,6144]{1,0:T(8,128)(2,1)S(1)}, bf16[16,6144]{1,0:T(8,128)(2,1)S(1)}, u32[]{:S(2)}, u32[]{:S(2)}) collective-permute-start(bf16[16,6144]{1,0:T(8,128)(2,1)S(1)} %collective-permute-done.1), channel_id=1, source_target_pairs={{0,2},{1,3},{2,0},{3,1},{4,6},{5,7},{6,4},{7,5},{8,10},{9,11},{10,... | collective-permute-start | bytes 589832 | tf_op jit(solution)/shard_map/ppermute | solution.py:64
  17.7 8.1 %collective-permute-start.6 = (bf16[16,6144]{1,0:T(8,128)(2,1)S(1)}, bf16[16,6144]{1,0:T(8,128)(2,1)S(1)}, u32[]{:S(2)}, u32[]{:S(2)}) collective-permute-start(bf16[16,6144]{1,0:T(8,128)(2,1)S(1)} %collective-permute-done.3), channel_id=1, source_target_pairs={{0,4},{1,5},{2,6},{3,7},{4,0},{5,1},{6,2},{7,3},{8,12},{9,13},{10,... | collective-permute-start | bytes 589832 | tf_op jit(solution)/shard_map/ppermute | solution.py:64
  20.7 7.1 %collective-permute-start.4 = (bf16[16,6144]{1,0:T(8,128)(2,1)S(1)}, bf16[16,6144]{1,0:T(8,128)(2,1)S(1)}, u32[]{:S(2)}, u32[]{:S(2)}) collective-permute-start(bf16[16,6144]{1,0:T(8,128)(2,1)S(1)} %collective-permute-done.3), channel_id=1, source_target_pairs={{0,2},{1,3},{2,0},{3,1},{4,6},{5,7},{6,4},{7,5},{8,10},{9,11},{10,... | collective-permute-start | bytes 589832 | tf_op jit(solution)/shard_map/ppermute | solution.py:64
  25.8 5.9 %copy-start.2 = (bf16[1536]{0:T(1024)(128)(2,1)S(1)}, bf16[1536]{0:T(1024)(128)(2,1)}, u32[]{:S(2)}) copy-start(bf16[1536]{0:T(1024)(128)(2,1)} %param.13) | copy-start | bytes 9220
  25.8 5.7 %collective-permute-start.7 = (bf16[16,6144]{1,0:T(8,128)(2,1)S(1)}, bf16[16,6144]{1,0:T(8,128)(2,1)S(1)}, u32[]{:S(2)}, u32[]{:S(2)}) collective-permute-start(bf16[16,6144]{1,0:T(8,128)(2,1)S(1)} %broadcast_select_fusion), channel_id=1, source_target_pairs={{0,2},{1,3},{2,0},{3,1},{4,6},{5,7},{6,4},{7,5},{8,10},{9,11},{10,... | collective-permute-start | bytes 589832 | tf_op jit(solution)/shard_map/ppermute | solution.py:64
  27.8 8.6 %collective-permute-start.9 = (bf16[32,6144]{1,0:T(8,128)(2,1)S(1)}, bf16[32,6144]{1,0:T(8,128)(2,1)S(1)}, u32[]{:S(2)}, u32[]{:S(2)}) collective-permute-start(bf16[32,6144]{1,0:T(8,128)(2,1)S(1)} %constant_dynamic-update-slice_fusion.refs_1_), channel_id=1, source_target_pairs={{0,1},{1,0},{2,3},{3,2},{4,5},{5,4},{6,7},{7,6},{8,9},{9,8},{10,11... | collective-permute-start | bytes 1179656 | tf_op jit(solution)/shard_map/ppermute | solution.py:64
  27.9 8.4 %collective-permute-start.8 = (bf16[64,6144]{1,0:T(8,128)(2,1)S(1)}, bf16[64,6144]{1,0:T(8,128)(2,1)S(1)}, u32[]{:S(2)}, u32[]{:S(2)}) collective-permute-start(bf16[64,6144]{1,0:T(8,128)(2,1)S(1)} %pad_maximum_fusion.refs_0_), channel_id=1, source_target_pairs={{0,1},{1,0},{2,3},{3,2},{4,5},{5,4},{6,7},{7,6},{8,9},{9,8},{10,11... | collective-permute-start | bytes 2359304 | tf_op jit(solution)/shard_map/ppermute | solution.py:64
  31.6 4.8 %collective-permute-start.10 = (bf16[32,6144]{1,0:T(8,128)(2,1)S(1)}, bf16[32,6144]{1,0:T(8,128)(2,1)S(1)}, u32[]{:S(2)}, u32[]{:S(2)}) collective-permute-start(bf16[32,6144]{1,0:T(8,128)(2,1)S(1)} %constant_dynamic-update-slice_fusion.2.refs_2_), channel_id=1, source_target_pairs={{0,1},{1,0},{2,3},{3,2},{4,5},{5,4},{6,7},{7,6},{8,9},{9,8},{10,11... | collective-permute-start | bytes 1179656 | tf_op jit(solution)/shard_map/ppermute | solution.py:64
  48.1 2.5 %collective-permute-start.12 = (f16[64,6144]{1,0:T(8,128)(2,1)S(1)}, f16[64,6144]{1,0:T(8,128)(2,1)S(1)}, u32[]{:S(2)}, u32[]{:S(2)}) collective-permute-start(f16[64,6144]{1,0:T(8,128)(2,1)S(1)} %convert_element_type.60), channel_id=1, source_target_pairs={{0,1},{1,0},{2,3},{3,2},{4,5},{5,4},{6,7},{7,6},{8,9},{9,8},{10,11... | collective-permute-start | bytes 2359304 | tf_op jit(solution)/shard_map/ppermute | solution.py:64
  48.8 3.6 %collective-permute-start.11 = (f16[64,6144]{1,0:T(8,128)(2,1)S(1)}, f16[64,6144]{1,0:T(8,128)(2,1)S(1)}, u32[]{:S(2)}, u32[]{:S(2)}) collective-permute-start(f16[64,6144]{1,0:T(8,128)(2,1)S(1)} %convert_element_type.58), channel_id=1, source_target_pairs={{0,1},{1,0},{2,3},{3,2},{4,5},{5,4},{6,7},{7,6},{8,9},{9,8},{10,11... | collective-permute-start | bytes 2359304 | tf_op jit(solution)/shard_map/ppermute | solution.py:64
  50.9 7.2 %collective-permute-start.13 = (f16[16,6144]{1,0:T(8,128)(2,1)S(1)}, f16[16,6144]{1,0:T(8,128)(2,1)S(1)}, u32[]{:S(2)}, u32[]{:S(2)}) collective-permute-start(f16[16,6144]{1,0:T(8,128)(2,1)S(1)} %get-tuple-element.52), channel_id=1, source_target_pairs={{0,2},{1,3},{2,0},{3,1},{4,6},{5,7},{6,4},{7,5},{8,10},{9,11},{10,... | collective-permute-start | bytes 589832 | tf_op jit(solution)/shard_map/ppermute | solution.py:64
  58.2 9.5 %collective-permute-start.17 = (f16[16,6144]{1,0:T(8,128)(2,1)S(1)}, f16[16,6144]{1,0:T(8,128)(2,1)S(1)}, u32[]{:S(2)}, u32[]{:S(2)}) collective-permute-start(f16[16,6144]{1,0:T(8,128)(2,1)S(1)} %fusion.2), channel_id=1, source_target_pairs={{0,4},{1,5},{2,6},{3,7},{4,0},{5,1},{6,2},{7,3},{8,12},{9,13},{10,... | collective-permute-start | bytes 589832 | tf_op jit(solution)/shard_map/ppermute | solution.py:64
  60.8 6.1 %collective-permute-start.14 = (f16[16,6144]{1,0:T(8,128)(2,1)S(1)}, f16[16,6144]{1,0:T(8,128)(2,1)S(1)}, u32[]{:S(2)}, u32[]{:S(2)}) collective-permute-start(f16[16,6144]{1,0:T(8,128)(2,1)S(1)} %get-tuple-element.40), channel_id=1, source_target_pairs={{0,2},{1,3},{2,0},{3,1},{4,6},{5,7},{6,4},{7,5},{8,10},{9,11},{10,... | collective-permute-start | bytes 589832 | tf_op jit(solution)/shard_map/ppermute | solution.py:64
  61.7 11.8 %collective-permute-start.19 = (f16[16,6144]{1,0:T(8,128)(2,1)S(1)}, f16[16,6144]{1,0:T(8,128)(2,1)S(1)}, u32[]{:S(2)}, u32[]{:S(2)}) collective-permute-start(f16[16,6144]{1,0:T(8,128)(2,1)S(1)} %fusion.2), channel_id=1, source_target_pairs={{4,8},{5,9},{6,10},{7,11},{8,4},{9,5},{10,6},{11,7},{20,24},{21,25... | collective-permute-start | bytes 589832 | tf_op jit(solution)/shard_map/ppermute | solution.py:64
  66.9 12.6 %copy-start = (bf16[16,6144]{1,0:T(8,128)(2,1)S(1)}, bf16[16,6144]{1,0:T(8,128)(2,1)}, u32[]{:S(2)}) copy-start(bf16[16,6144]{1,0:T(8,128)(2,1)} %adjoint_ref.1) | copy-start | bytes 589828
  66.9 12.6 %copy-start.1 = (f32[6144]{0:T(1024)S(1)}, f32[6144]{0:T(1024)}, u32[]{:S(2)}) copy-start(f32[6144]{0:T(1024)} %param.11) | copy-start | bytes 73732
  66.9 5.8 %collective-permute-start.15 = (f16[16,6144]{1,0:T(8,128)(2,1)S(1)}, f16[16,6144]{1,0:T(8,128)(2,1)S(1)}, u32[]{:S(2)}, u32[]{:S(2)}) collective-permute-start(f16[16,6144]{1,0:T(8,128)(2,1)S(1)} %get-tuple-element.41), channel_id=1, source_target_pairs={{0,2},{1,3},{2,0},{3,1},{4,6},{5,7},{6,4},{7,5},{8,10},{9,11},{10,... | collective-permute-start | bytes 589832 | tf_op jit(solution)/shard_map/ppermute | solution.py:64
  67.8 8.3 %collective-permute-start.18 = (f16[16,6144]{1,0:T(8,128)(2,1)S(1)}, f16[16,6144]{1,0:T(8,128)(2,1)S(1)}, u32[]{:S(2)}, u32[]{:S(2)}) collective-permute-start(f16[16,6144]{1,0:T(8,128)(2,1)S(1)} %fusion.4), channel_id=1, source_target_pairs={{0,12},{1,13},{2,14},{3,15},{4,8},{5,9},{6,10},{7,11},{8,4},{9,5},... | collective-permute-start | bytes 589832 | tf_op jit(solution)/shard_map/ppermute | solution.py:64
  72.7 5.7 %collective-permute-start.16 = (f16[16,6144]{1,0:T(8,128)(2,1)S(1)}, f16[16,6144]{1,0:T(8,128)(2,1)S(1)}, u32[]{:S(2)}, u32[]{:S(2)}) collective-permute-start(f16[16,6144]{1,0:T(8,128)(2,1)S(1)} %get-tuple-element.42), channel_id=1, source_target_pairs={{0,2},{1,3},{2,0},{3,1},{4,6},{5,7},{6,4},{7,5},{8,10},{9,11},{10,... | collective-permute-start | bytes 589832 | tf_op jit(solution)/shard_map/ppermute | solution.py:64
  73.6 5.8 %collective-permute-start.20 = (f16[16,6144]{1,0:T(8,128)(2,1)S(1)}, f16[16,6144]{1,0:T(8,128)(2,1)S(1)}, u32[]{:S(2)}, u32[]{:S(2)}) collective-permute-start(f16[16,6144]{1,0:T(8,128)(2,1)S(1)} %fusion.1), channel_id=1, source_target_pairs={{0,4},{1,5},{2,6},{3,7},{4,0},{5,1},{6,2},{7,3},{8,12},{9,13},{10,... | collective-permute-start | bytes 589832 | tf_op jit(solution)/shard_map/ppermute | solution.py:64

commit v3 on v2

--- a/solution.py
+++ b/solution.py
@@ -49,15 +49,10 @@
     return finish(lax.dynamic_slice_in_dim(latent, start, own_rows, 0), adjoint, scale_row, d_hidden)
 
 
-def middle(i):
-    return (i >> 2) in (1, 2)
-
-
 CORE = [(i, i ^ 1) for i in range(16)]
 SIDE = [(i, i ^ 2) for i in range(16)]
 PAIR = [(i, i ^ 4) for i in range(16)]
 CROSS = [(i, i ^ 12) for i in range(16)]
-CROSS_MID = [(i, i ^ 12) for i in range(16) if middle(i)]
 
 
 def send(x, pairs):
@@ -76,23 +71,25 @@
     return lax.optimization_barrier((x, *done))[0]
 
 
-def scatter_sums(quarters, is_mid, rows):
-    near_early, near_late, far_early, far_late = quarters
-    late = near_late + wide(send(half(far_late), CORE))
-    p30, p31, p20, p21 = [late[k * rows : (k + 1) * rows] for k in range(4)]
-    y2 = send(half(p21), SIDE)
-    early = near_early + wide(send(half(far_early), CORE))
-    p00, p01, p10, p11 = [early[k * rows : (k + 1) * rows] for k in range(4)]
-    p20 = p20 + wide(y2)
-    a2 = send(half(p20), PAIR)
-    m2 = send(half(p20), CROSS_MID)
-    y3 = send(after(half(p31), y2), SIDE)
-    y1 = send(after(half(p11), y3), SIDE)
-    p30 = p30 + wide(y3) + jnp.where(is_mid, wide(a2), 0.0)
-    x = send(half(p30), CROSS)
-    y0 = send(after(half(p01), y1), SIDE)
-    a1 = send(half(p10 + wide(y1) + wide(m2)), PAIR)
-    return p00 + wide(y0) + wide(x) + wide(a1)
+def scatter_sums(chunks, rows):
+    cut = lambda x, k: x[k * rows : (k + 1) * rows]
+    sums = []
+    for near_early, near_late, far_early, far_late in chunks:
+        c_late = send(half(far_late), CORE)
+        c_early = send(half(far_early), CORE)
+        late = near_late + wide(c_late)
+        early = near_early + wide(c_early)
+        p00, p01, p10, p11 = [cut(early, k) for k in range(4)]
+        p30, p31, p20, p21 = [cut(late, k) for k in range(4)]
+        z21 = send(half(p21), PAIR)
+        y1 = send(half(p11), SIDE)
+        y3 = send(half(p31 + wide(z21)), SIDE)
+        z20 = send(half(p20), PAIR)
+        z3 = send(half(p30 + wide(y3) + wide(z20)), CROSS)
+        z1 = send(after(half(p10 + wide(y1)), z20), PAIR)
+        y0 = send(after(half(p01), y3), SIDE)
+        sums.append(p00 + wide(y0) + wide(z1) + wide(z3))
+    return sums
 
 
 VMEM = pl.BlockSpec(memory_space=pltpu.VMEM)
@@ -146,66 +143,88 @@
     lax.fori_loop(1, 16, step, 0, unroll=3)
 
 
-def add_products(acc, start, h_ref, copies, w_buf):
-    n = w_buf.shape[1]
-    for k, copy in enumerate(copies):
-        copy.wait()
-        product = jnp.dot(h_ref[:, start + k * n : start + (k + 1) * n], w_buf[k], preferred_element_type=jnp.float32)
-        acc = product if acc is None else acc + product
-    return acc
-
-
-def first_kernel(rows, me_ref, latent_ref, shift_ref, scale_ref, wu_ref, wd_ref, h_ref, own_ref, rstd_ref, u_ref, wd_out, latent_buf, shift_buf, scale_buf, w_buf, sems, w_sems, wd_sem):
+def add_product(acc, at, h_ref, w):
+    product = jnp.dot(h_ref[:, at : at + w.shape[0]], w, preferred_element_type=jnp.float32)
+    return product if acc is None else acc + product
+
+
+def first_kernel(rows, me_ref, latent_ref, shift_ref, scale_ref, wu_ref, wd_ref, h_ref, own_ref, rstd_ref, u_ref, next_ref, wd_out, latent_buf, shift_buf, scale_buf, w_buf, sems, w_sems, out_sems):
     copies = [
         load(source, target, sems.at[k])
         for k, (source, target) in enumerate([(latent_ref, latent_buf), (shift_ref, shift_buf), (scale_ref, scale_buf)])
     ]
+    n = w_buf.shape[1]
     w_copies = load_parts(wu_ref, 0, w_buf, w_sems)
-    wd_copy = load(wd_ref.at[pl.ds(0, wd_out.shape[0])], wd_out, wd_sem)
+    outs = [
+        load(wu_ref.at[pl.ds(2 * n, n)], next_ref, out_sems.at[0]),
+        load(wd_ref.at[pl.ds(0, wd_out.shape[0])], wd_out, out_sems.at[1]),
+    ]
     for copy in copies:
         copy.wait()
     normalize_rows(rows, me_ref, latent_buf, shift_buf, scale_buf, h_ref, own_ref, rstd_ref)
-    u_ref[...] = add_products(None, 0, h_ref, w_copies, w_buf)
-    wd_copy.wait()
-
-
-def second_kernel(start, h_ref, u_ref, wu_ref, u_out, w_buf, w_sems):
-    u_out[...] = add_products(u_ref[...], start, h_ref, load_parts(wu_ref, start, w_buf, w_sems), w_buf)
-
-
-def third_kernel(start, h_ref, u_ref, b_ref, wu_ref, slope_out, w_buf, w_sems):
-    second_kernel(start, h_ref, u_ref, wu_ref, slope_out, w_buf, w_sems)
+    u = None
+    for k, copy in enumerate(w_copies):
+        copy.wait()
+        u = add_product(u, k * n, h_ref, w_buf[k])
+    u_ref[...] = u
+    for copy in outs:
+        copy.wait()
+
+
+def second_kernel(start, h_ref, u_ref, w_ref, wu_ref, u_out, next_ref, w_buf, sems):
+    n = w_buf.shape[0]
+    copy = load(wu_ref.at[pl.ds(start + n, n)], w_buf, sems.at[0])
+    ahead = load(wu_ref.at[pl.ds(start + 2 * n, n)], next_ref, sems.at[1])
+    u = add_product(u_ref[...], start, h_ref, w_ref[...])
+    copy.wait()
+    u_out[...] = add_product(u, start + n, h_ref, w_buf[...])
+    ahead.wait()
+
+
+def third_kernel(start, h_ref, u_ref, w_ref, b_ref, wu_ref, wd_ref, slope_out, wd_out, w_buf, sems):
+    n = w_buf.shape[0]
+    copy = load(wu_ref.at[pl.ds(start + n, n)], w_buf, sems.at[0])
+    ahead = load(wd_ref.at[pl.ds(wd_out.shape[0], wd_out.shape[0])], wd_out, sems.at[1])
+    u = add_product(u_ref[...], start, h_ref, w_ref[...])
+    copy.wait()
+    slope_out[...] = add_product(u, start + n, h_ref, w_buf[...])
     width = slope_out.shape[1] // 3
     for j in range(3):
         cut = slice(j * width, (j + 1) * width)
         slope_out[:, cut] = gelu_slope(slope_out[:, cut] + b_ref[:, cut].astype(jnp.float32))
+    ahead.wait()
 
 
 def du_kernel(*refs):
-    pieces, (wd_early, slope_ref, wd_ref, wu_ref), (du_ref, unit_ref, wu_out, wd_buf, sems) = refs[:6], refs[6:10], refs[10:]
-    early, late = wd_early.shape[0], wd_buf.shape[0]
-    wd_copy = load(wd_ref.at[pl.ds(early, late)], wd_buf, sems.at[0])
+    pieces, (wd0_ref, wd1_ref, slope_ref, wd_ref, wu_ref, du_ref, unit_ref, wu_out, wd_buf, sems) = refs[:6], refs[6:]
+    width, at = wd_buf.shape[0], 0
+    wd_copy = load(wd_ref.at[pl.ds(2 * width, width)], wd_buf, sems.at[0])
     wu_copy = load(wu_ref.at[pl.ds(0, wu_out.shape[0])], wu_out, sems.at[1])
-    at = 0
     for piece in pieces:
         top = jnp.max(jnp.abs(piece[...].astype(jnp.float32)), axis=1, keepdims=True)
         unit_ref[at : at + piece.shape[0], :] = 16.0 * jnp.maximum(top, 1e-30)
         at += piece.shape[0]
     gated = jnp.concatenate([piece[...] for piece in pieces], axis=0)
-    for at in range(0, early + late, late):
-        if at == early:
+    for k, wd in enumerate((wd0_ref, wd1_ref, wd_buf)):
+        if k == 2:
             wd_copy.wait()
-        wd = wd_early[at : at + late, :] if at < early else wd_buf[...]
-        du_ref[:, at : at + late] = (rows_t(gated, wd) * slope_ref[:, at : at + late]).astype(du_ref.dtype)
+        cut = slice(k * width, (k + 1) * width)
+        du_ref[:, cut] = (rows_t(gated, wd[...]) * slope_ref[:, cut]).astype(du_ref.dtype)
     wu_copy.wait()
 
 
-def dh_kernel(du_ref, unit_ref, early_ref, wu_ref, *refs):
-    outs, (w_buf, sems) = refs[:-2], refs[-2:]
+def dh_kernel(start, ahead, du_ref, unit_ref, early_ref, wu_ref, *refs):
+    outs, refs = refs[:4], refs[4:]
+    if ahead:
+        ahead_out, w_buf, sems, ahead_sem = refs
+    else:
+        w_buf, sems = refs
     n, early, width = outs[0].shape[0], early_ref.shape[0], w_buf.shape[1]
-    copies = load_parts(wu_ref, early, w_buf, sems)
+    copies = load_parts(wu_ref, start + early, w_buf, sems)
+    if ahead:
+        ahead_copy = load(wu_ref.at[pl.ds(start + outs[0].shape[1], ahead)], ahead_out, ahead_sem)
     scale = 1.0 / unit_ref[...]
-    for at in range(0, wu_ref.shape[0], width):
+    for at in range(0, outs[0].shape[1], width):
         if at < early:
             w = early_ref[at : at + width, :]
         else:
@@ -215,6 +234,8 @@
         dh = rows_t(du_ref[...], w) * scale
         for j, out in enumerate(outs):
             out[:, at : at + width] = dh[j * n : (j + 1) * n]
+    if ahead:
+        ahead_copy.wait()
 
 
 def finish_kernel(sum_ref, unit_ref, own_ref, rstd_ref, scale_ref, adjoint_ref, out_ref):
@@ -230,8 +251,6 @@
     rows, d = adjoint.shape
     tokens, ff = latent.shape[0], w_up.shape[1]
     me = lax.axis_index("fsdp")
-    z = me >> 2
-    is_mid = (z == 1) | (z == 2)
     f32, bf16 = jnp.float32, jnp.bfloat16
     work = 2 * tokens * d * ff
     shape = jax.ShapeDtypeStruct
@@ -244,66 +263,70 @@
     b10 = send(b00, PAIR)
     b01 = send(b00, SIDE)
 
-    third, depth = ff // 3, d // 6
-    u_shape = shape((tokens, ff), f32)
-    w_scratch = [pltpu.VMEM((2, depth, ff), bf16)]
-    w_sems = [pltpu.SemaphoreType.DMA((2,))]
-    h, own_normed, own_rstd, u, wd_early = kernel(
+    depth, third = d // 6, ff // 3
+    wd_shape = shape((third, d), bf16)
+    u_shape, part_shape = shape((tokens, ff), f32), shape((depth, ff), bf16)
+    part = pltpu.VMEM((depth, ff), bf16)
+    sems = lambda n: pltpu.SemaphoreType.DMA((n,))
+    h, own_normed, own_rstd, u, part2, wd0 = kernel(
         functools.partial(first_kernel, rows),
         [SMEM] + [HBM] * 5,
-        [shape((tokens, d), bf16), shape((rows, d), f32), shape((rows, 1), f32), u_shape, shape((2 * third, d), bf16)],
-        work // 2, 4 * d * third, 18,
+        [shape((tokens, d), bf16), shape((rows, d), f32), shape((rows, 1), f32), u_shape, part_shape, wd_shape],
+        work // 2, 2 * d * ff, 18,
         scratch_shapes=[pltpu.VMEM((tokens, d), bf16), pltpu.VMEM((1, d), f32), pltpu.VMEM((1, d), f32)]
-        + w_scratch + [pltpu.SemaphoreType.DMA((3,))] + w_sems + [pltpu.SemaphoreType.DMA],
+        + [pltpu.VMEM((2, depth, ff), bf16), sems(3), sems(2), sems(2)],
     )(me.reshape(1).astype(jnp.int32), stay(latent), stay(shift_row[None]), stay(scale), w_up, w_down)
 
     b10, b30 = after(b10, u), after(b30, u)
-    m2 = send(b10, CROSS_MID)
-    a2 = send(b30, PAIR)
-    b11 = send(b10, SIDE)
     b31 = send(b30, SIDE)
-    u = kernel(
+    b20 = send(b30, PAIR)
+    u, part4 = kernel(
         functools.partial(second_kernel, 2 * depth),
-        [VMEM] * 2 + [HBM],
-        u_shape,
-        work // 3, 2 * d * third, 12,
-        scratch_shapes=w_scratch + w_sems,
-    )(h, after(u, b10, b30), w_up)
-
-    b20 = after(jnp.where(is_mid, m2, a2), u)
-    b21 = send(b20, SIDE)
-    slope = kernel(
+        [VMEM] * 3 + [HBM],
+        [u_shape, part_shape],
+        work // 3, d * ff, 12,
+        scratch_shapes=[part, sems(2)],
+    )(h, after(u, b30), part2, w_up)
+
+    b31 = after(b31, u)
+    b21 = send(b31, PAIR)
+    b11 = send(after(b10, b31), SIDE)
+    slope, wd1 = kernel(
         functools.partial(third_kernel, 4 * depth),
-        [VMEM] * 3 + [HBM],
-        u_shape,
-        work // 3, 2 * d * third, 12,
-        scratch_shapes=w_scratch + w_sems,
-    )(h, after(u, b20), b_up[None], w_up)
-
+        [VMEM] * 4 + [HBM] * 2,
+        [u_shape, wd_shape],
+        work // 3, d * ff, 12,
+        scratch_shapes=[part, sems(2)],
+    )(h, after(u, b31), part4, b_up[None], w_up, w_down)
+
+    b11, b21 = after(b11, slope), after(b21, slope)
     cat = lambda *blocks: jnp.concatenate(blocks, axis=0)
+    c0, c13, c32 = [send(cat(*x), CORE) for x in ((b00, b01), (b10, b30), (b31, b20))]
+    c11, c21 = send(b11, CORE), send(b21, CORE)
     pieces = [cat(b00, b01, b10, b11), cat(b30, b31), cat(b20, b21)]
-    pieces = pieces + [send(x, CORE) for x in pieces]
+    pieces += [cat(c0, c13[:rows], c11), cat(c13[rows:], c32[:rows]), cat(c32[rows:], c21)]
     early = 2 * depth
     du, unit, wu_early = kernel(
         du_kernel,
-        [VMEM] * 8 + [HBM] * 2,
+        [VMEM] * 9 + [HBM] * 2,
         [shape((tokens, ff), bf16), shape((tokens, 1), f32), shape((early, ff), bf16)],
         work, 2 * d * ff, 16,
-        scratch_shapes=[pltpu.VMEM((third, d), bf16), pltpu.SemaphoreType.DMA((2,))],
-    )(*pieces, wd_early, slope, w_down, w_up)
+        scratch_shapes=[pltpu.VMEM((third, d), bf16), sems(2)],
+    )(*pieces, wd0, wd1, slope, w_down, w_up)
     quarters = kernel(
-        dh_kernel,
+        functools.partial(dh_kernel, 0, 0),
         [VMEM] * 3 + [HBM],
         [shape((tokens // 4, d), f32)] * 4,
         work, 2 * d * ff, 20,
         scratch_shapes=[pltpu.VMEM((4, depth, ff), bf16), pltpu.SemaphoreType.DMA((4,))],
     )(du, unit, wu_early, w_up)
+    (total,) = scatter_sums([quarters], rows)
     return kernel(
         finish_kernel,
         [VMEM] * 6,
         shape((rows, d), f32),
         20 * rows * d, 10 * rows * d, 8,
-    )(scatter_sums(quarters, is_mid, rows), unit, own_normed, own_rstd, scale, adjoint)
+    )(total, unit, own_normed, own_rstd, scale, adjoint)
 
 
 def solution(mesh):

time: 80.7 us -> 72.7 us (0.901)
  waiting for transfers between devices: 23.6 us -> 17.8 us
  starting transfers between devices: 25.2 us -> 23.9 us
  Pallas kernels: 29.3 us -> 28.3 us
    ppermute x21, waiting for transfers between devices: 23.6 us -> 17.8 us  [send(): return lax.ppermute(x, 'fsdp', pairs)]
    pallas_call x4, Pallas kernels: 20.1 us -> 18.3 us  [the longest x1 6.16 us: line_of_four(): kernel(functools.partial(dh_kernel, 0, 0), [VMEM] * 3 + [HBM], [shape((to...]
    ppermute x21, starting transfers between devices: 25.2 us -> 23.9 us  [send(): return lax.ppermute(x, 'fsdp', pairs)]
    pallas_call x1, Pallas kernels: 8.05 us -> 8.97 us  [line_of_four(): kernel(functools.partial(first_kernel, rows), [SMEM] + [HBM] * 5, [shape(...]
  transfers between devices with their start and end apart: 21 -> 21, of which waited for: 9 -> 9; matrix products, arithmetic and copies ran while one was open for 1% -> 2% of each run, Pallas kernels for 21% -> 22%
where the time goes in v3:
time: 72.7 us; the launch traced here: 72.6 us
  Pallas kernels  28.3 us (39%)
  starting transfers between devices  23.9 us (33%)
  waiting for transfers between devices  17.8 us (24%)
  other arithmetic  2.17 us (3%)
    ppermute x21, starting transfers between devices, send(): return lax.ppermute(x, 'fsdp', pairs)  23.9 us
    ppermute x21, waiting for transfers between devices, send(): return lax.ppermute(x, 'fsdp', pairs)  17.8 us
    pallas_call x1, Pallas kernels, line_of_four(): kernel(functools.partial(first_kernel, rows), [SMEM] + [HBM] * 5, [shape(...  8.97 us
    pallas_call x1, Pallas kernels, line_of_four(): kernel(functools.partial(dh_kernel, 0, 0), [VMEM] * 3 + [HBM], [shape((to...  6.16 us
    pallas_call x1, Pallas kernels, line_of_four(): kernel(du_kernel, [VMEM] * 9 + [HBM] * 2, [shape((tokens, ff), bf16), sha...  5.44 us
    pallas_call x1, Pallas kernels, line_of_four(): kernel(functools.partial(third_kernel, 4 * depth), [VMEM] * 4 + [HBM] * 2...  3.78 us
    pallas_call x1, Pallas kernels, line_of_four(): kernel(functools.partial(second_kernel, 2 * depth), [VMEM] * 3 + [HBM], [...  2.91 us
  transfers between devices with their start and end apart: 21, of which 9 were waited for; matrix products, arithmetic and copies ran while one was open for 2% of the time, Pallas kernels for 22%

profile of v3, /device:TPU:0, one launch (start us, length us, event | category | flops | bytes accessed | tf_op | source)
XLA Modules:
  0.0 72.6 jit_solution(15017984209314042478)
XLA Ops:
  0.0 1.0 %multiply_convert_fusion = bf16[16,6144]{1,0:T(8,128)(2,1)S(1)} fusion(bf16[16,6144]{1,0:T(8,128)(2,1)} %adjoint_ref.1, f32[6144]{0:T(1024)} %param.12), kind=kLoop, calls=%fused_computation.21 | loop fusion | flops 294912 | bytes 417792 | tf_op jit(solution)/shard_map/convert_element_type | solution.py:261
  1.0 5.1 %collective-permute-start.2 = (bf16[16,6144]{1,0:T(8,128)(2,1)S(1)}, bf16[16,6144]{1,0:T(8,128)(2,1)S(1)}, u32[]{:S(2)}, u32[]{:S(2)}) collective-permute-start(bf16[16,6144]{1,0:T(8,128)(2,1)S(1)} %multiply_convert_fusion), channel_id=1, source_target_pairs={{0,12},{1,13},{2,14},{3,15},{4,8},{5,9},{6,10},{7,11},{8,4},{9,5},... | collective-permute-start | bytes 589832 | tf_op jit(solution)/shard_map/ppermute | solution.py:59
  6.1 9.0 %shard_map.82 = (bf16[256,6144]{1,0:T(8,128)(2,1)S(1)}, f32[16,6144]{1,0:T(8,128)S(1)}, f32[16,1]{1,0:T(8,128)S(1)}, f32[256,1536]{1,0:T(8,128)S(1)}, bf16[1024,...) custom-call(s32[1]{0:T(128)} %bitcast.me_ref, bf16[256,6144]{1,0:T(8,128)(2,1)} %latent_ref.1, f32[1,6144]{1,0:T(1,128)} %bitcast.5, ...), custom_call_target="tpu_custom_call" | custom-call | flops 2415919104 | bytes 18874368 | tf_op jit(solution)/shard_map/pallas_call | solution.py:271
  15.1 1.6 %collective-permute-start.3 = (bf16[16,6144]{1,0:T(8,128)(2,1)S(1)}, bf16[16,6144]{1,0:T(8,128)(2,1)S(1)}, u32[]{:S(2)}, u32[]{:S(2)}) collective-permute-start(bf16[16,6144]{1,0:T(8,128)(2,1)S(1)} %collective-permute-done.2), channel_id=1, source_target_pairs={{0,2},{1,3},{2,0},{3,1},{4,6},{5,7},{6,4},{7,5},{8,10},{9,11},{10,... | collective-permute-start | bytes 589832 | tf_op jit(solution)/shard_map/ppermute | solution.py:59
  16.7 0.5 collective-permute-start
  17.2 2.1 %collective-permute-start.5 = (bf16[16,6144]{1,0:T(8,128)(2,1)S(1)}, bf16[16,6144]{1,0:T(8,128)(2,1)S(1)}, u32[]{:S(2)}, u32[]{:S(2)}) collective-permute-start(bf16[16,6144]{1,0:T(8,128)(2,1)S(1)} %collective-permute-done.2), channel_id=1, source_target_pairs={{0,4},{1,5},{2,6},{3,7},{4,0},{5,1},{6,2},{7,3},{8,12},{9,13},{10,... | collective-permute-start | bytes 589832 | tf_op jit(solution)/shard_map/ppermute | solution.py:59
  19.3 2.9 %shard_map.83 = (f32[256,1536]{1,0:T(8,128)S(1)}, bf16[1024,1536]{1,0:T(8,128)(2,1)S(1)}) custom-call(bf16[256,6144]{1,0:T(8,128)(2,1)S(1)} %get-tuple-element.35.h_ref, f32[256,1536]{1,0:T(8,128)S(1)} %get-tuple-element.36.u_ref, bf16[1024,1536]{1,0:T(8,128)(2,1)S(1)} %get-tuple-element.37.w_ref, bf16[6144,1536]{1,0:T(8,128)(2,1)} %wu_ref.7), custom_call_target="tpu_custom_call" | custom-call | flops 1610612736 | bytes 9437184 | tf_op jit(solution)/shard_map/pallas_call | solution.py:283
  22.2 0.8 %collective-permute-done.3 = bf16[16,6144]{1,0:T(8,128)(2,1)S(1)} collective-permute-done((bf16[16,6144]{1,0:T(8,128)(2,1)S(1)}, bf16[16,6144]{1,0:T(8,128)(2,1)S(1)}, u32[]{:S(2)}, u32[]{:S(2)}) %collective-permute-start.3) | collective-permute-done | bytes 196640 | tf_op jit(solution)/shard_map/ppermute | solution.py:59
  23.0 2.0 %collective-permute-start.6 = (bf16[16,6144]{1,0:T(8,128)(2,1)S(1)}, bf16[16,6144]{1,0:T(8,128)(2,1)S(1)}, u32[]{:S(2)}, u32[]{:S(2)}) collective-permute-start(bf16[16,6144]{1,0:T(8,128)(2,1)S(1)} %collective-permute-done.3), channel_id=1, source_target_pairs={{0,4},{1,5},{2,6},{3,7},{4,0},{5,1},{6,2},{7,3},{8,12},{9,13},{10,... | collective-permute-start | bytes 589832 | tf_op jit(solution)/shard_map/ppermute | solution.py:59
  25.0 1.5 %collective-permute-start.4 = (bf16[16,6144]{1,0:T(8,128)(2,1)S(1)}, bf16[16,6144]{1,0:T(8,128)(2,1)S(1)}, u32[]{:S(2)}, u32[]{:S(2)}) collective-permute-start(bf16[16,6144]{1,0:T(8,128)(2,1)S(1)} %collective-permute-done.1), channel_id=1, source_target_pairs={{0,2},{1,3},{2,0},{3,1},{4,6},{5,7},{6,4},{7,5},{8,10},{9,11},{10,... | collective-permute-start | bytes 589832 | tf_op jit(solution)/shard_map/ppermute | solution.py:59
  26.5 0.7 collective-permute-done
  27.2 0.1 collective-permute-start.7
  27.3 3.8 %shard_map.84 = (f32[256,1536]{1,0:T(8,128)S(1)}, bf16[512,6144]{1,0:T(8,128)(2,1)S(1)}) custom-call(bf16[256,6144]{1,0:T(8,128)(2,1)S(1)} %get-tuple-element.35.h_ref, f32[256,1536]{1,0:T(8,128)S(1)} %get-tuple-element.41.u_ref, bf16[1024,1536]{1,0:T(8,128)(2,1)S(1)} %get-tuple-element.42.w_ref, bf16[1,1536]{1,0:T(2,128)(2,1)S(1)} %broadcast_in_dim.12.b_ref, ...), custom_call_target="tpu_custom_call" | custom-call | flops 1610612736 | bytes 9437184 | tf_op jit(solution)/shard_map/pallas_call | solution.py:294
  31.1 0.6 collective-permute-start.9
  31.7 0.1 collective-permute-start.11
  31.7 0.1 pad_maximum_fusion.6
  31.9 0.5 collective-permute-start.10
  32.4 0.1 collective-permute-start.8
  32.5 1.2 %collective-permute-done.10 = bf16[32,6144]{1,0:T(8,128)(2,1)S(1)} collective-permute-done((bf16[32,6144]{1,0:T(8,128)(2,1)S(1)}, bf16[32,6144]{1,0:T(8,128)(2,1)S(1)}, u32[]{:S(2)}, u32[]{:S(2)}) %collective-permute-start.10) | collective-permute-done | bytes 393248 | tf_op jit(solution)/shard_map/ppermute | solution.py:59
  33.7 0.5 collective-permute-done.8
  34.4 0.1 pad_maximum_fusion.1.refs_3_
  34.5 5.4 %shard_map.85 = (bf16[256,1536]{1,0:T(8,128)(2,1)S(1)}, f32[256,1]{1,0:T(8,128)S(1)}, bf16[2048,1536]{1,0:T(8,128)(2,1)S(1)}) custom-call(bf16[64,6144]{1,0:T(8,128)(2,1)S(1)} %pad_maximum_fusion.refs_0_, bf16[32,6144]{1,0:T(8,128)(2,1)S(1)} %get-tuple-element.72.refs_1_, bf16[32,6144]{1,0:T(8,128)(2,1)S(1)} %get-tuple-element.74.refs_2_, ...), custom_call_target="tpu_custom_call" | custom-call | flops 4831838208 | bytes 18874368 | tf_op jit(solution)/shard_map/pallas_call | solution.py:309
  39.9 6.2 %shard_map.86 = (f32[64,6144]{1,0:T(8,128)S(1)}, f32[64,6144]{1,0:T(8,128)S(1)}, f32[64,6144]{1,0:T(8,128)S(1)}, f32[64,6144]{1,0:T(8,128)S(1)}) custom-call(bf16[256,1536]{1,0:T(8,128)(2,1)S(1)} %get-tuple-element.48.du_ref, f32[256,1]{1,0:T(8,128)S(1)} %get-tuple-element.49.unit_ref, bf16[2048,1536]{1,0:T(8,128)(2,1)S(1)} %get-tuple-element.50.early_ref, ...), custom_call_target="tpu_custom_call" | custom-call | flops 4831838208 | bytes 18874368 | tf_op jit(solution)/shard_map/pallas_call | solution.py:316
  46.1 0.1 convert_element_type.56
  46.2 0.4 collective-permute-start.13
  46.6 0.1 convert_element_type.54
  46.7 0.2 collective-permute-start.12
  46.9 1.6 %collective-permute-done.13 = f16[64,6144]{1,0:T(8,128)(2,1)S(1)} collective-permute-done((f16[64,6144]{1,0:T(8,128)(2,1)S(1)}, f16[64,6144]{1,0:T(8,128)(2,1)S(1)}, u32[]{:S(2)}, u32[]{:S(2)}) %collective-permute-start.13) | collective-permute-done | bytes 786464 | tf_op jit(solution)/shard_map/ppermute | solution.py:59
  48.5 0.2 fusion.7
  48.7 0.1 fusion.9
  48.8 2.1 %collective-permute-start.14 = (f16[16,6144]{1,0:T(8,128)(2,1)S(1)}, f16[16,6144]{1,0:T(8,128)(2,1)S(1)}, u32[]{:S(2)}, u32[]{:S(2)}) collective-permute-start(f16[16,6144]{1,0:T(8,128)(2,1)S(1)} %get-tuple-element.65), channel_id=1, source_target_pairs={{0,4},{1,5},{2,6},{3,7},{4,0},{5,1},{6,2},{7,3},{8,12},{9,13},{10,... | collective-permute-start | bytes 589832 | tf_op jit(solution)/shard_map/ppermute | solution.py:59
  50.9 0.1 collective-permute-start.18
  51.0 0.2 fusion.6
  51.2 0.1 fusion.8
  51.3 1.6 %collective-permute-start.17 = (f16[16,6144]{1,0:T(8,128)(2,1)S(1)}, f16[16,6144]{1,0:T(8,128)(2,1)S(1)}, u32[]{:S(2)}, u32[]{:S(2)}) collective-permute-start(f16[16,6144]{1,0:T(8,128)(2,1)S(1)} %get-tuple-element.64), channel_id=1, source_target_pairs={{0,2},{1,3},{2,0},{3,1},{4,6},{5,7},{6,4},{7,5},{8,10},{9,11},{10,... | collective-permute-start | bytes 589832 | tf_op jit(solution)/shard_map/ppermute | solution.py:59
  52.9 3.8 %collective-permute-done.14 = f16[16,6144]{1,0:T(8,128)(2,1)S(1)} collective-permute-done((f16[16,6144]{1,0:T(8,128)(2,1)S(1)}, f16[16,6144]{1,0:T(8,128)(2,1)S(1)}, u32[]{:S(2)}, u32[]{:S(2)}) %collective-permute-start.14) | collective-permute-done | bytes 196640 | tf_op jit(solution)/shard_map/ppermute | solution.py:59
  56.7 0.1 fusion.3
  56.7 1.6 %collective-permute-start.15 = (f16[16,6144]{1,0:T(8,128)(2,1)S(1)}, f16[16,6144]{1,0:T(8,128)(2,1)S(1)}, u32[]{:S(2)}, u32[]{:S(2)}) collective-permute-start(f16[16,6144]{1,0:T(8,128)(2,1)S(1)} %fusion.3), channel_id=1, source_target_pairs={{0,2},{1,3},{2,0},{3,1},{4,6},{5,7},{6,4},{7,5},{8,10},{9,11},{10,... | collective-permute-start | bytes 589832 | tf_op jit(solution)/shard_map/ppermute | solution.py:59
  58.3 0.1 fusion.2
  58.4 2.2 %collective-permute-done.18 = f16[16,6144]{1,0:T(8,128)(2,1)S(1)} collective-permute-done((f16[16,6144]{1,0:T(8,128)(2,1)S(1)}, f16[16,6144]{1,0:T(8,128)(2,1)S(1)}, u32[]{:S(2)}, u32[]{:S(2)}) %collective-permute-start.18) | collective-permute-done | bytes 196640 | tf_op jit(solution)/shard_map/ppermute | solution.py:59
  60.6 1.7 %collective-permute-start.19 = (f16[16,6144]{1,0:T(8,128)(2,1)S(1)}, f16[16,6144]{1,0:T(8,128)(2,1)S(1)}, u32[]{:S(2)}, u32[]{:S(2)}) collective-permute-start(f16[16,6144]{1,0:T(8,128)(2,1)S(1)} %fusion.2), channel_id=1, source_target_pairs={{0,4},{1,5},{2,6},{3,7},{4,0},{5,1},{6,2},{7,3},{8,12},{9,13},{10,... | collective-permute-start | bytes 589832 | tf_op jit(solution)/shard_map/ppermute | solution.py:59
  62.3 0.8 %collective-permute-done.15 = f16[16,6144]{1,0:T(8,128)(2,1)S(1)} collective-permute-done((f16[16,6144]{1,0:T(8,128)(2,1)S(1)}, f16[16,6144]{1,0:T(8,128)(2,1)S(1)}, u32[]{:S(2)}, u32[]{:S(2)}) %collective-permute-start.15) | collective-permute-done | bytes 196640 | tf_op jit(solution)/shard_map/ppermute | solution.py:59
  63.1 0.1 fusion.1
  63.2 0.5 collective-permute-start.20
  63.6 1.5 %collective-permute-start.16 = (f16[16,6144]{1,0:T(8,128)(2,1)S(1)}, f16[16,6144]{1,0:T(8,128)(2,1)S(1)}, u32[]{:S(2)}, u32[]{:S(2)}) collective-permute-start(f16[16,6144]{1,0:T(8,128)(2,1)S(1)} %get-tuple-element.55), channel_id=1, source_target_pairs={{0,2},{1,3},{2,0},{3,1},{4,6},{5,7},{6,4},{7,5},{8,10},{9,11},{10,... | collective-permute-start | bytes 589832 | tf_op jit(solution)/shard_map/ppermute | solution.py:59
  65.1 6.2 %collective-permute-done.19 = f16[16,6144]{1,0:T(8,128)(2,1)S(1)} collective-permute-done((f16[16,6144]{1,0:T(8,128)(2,1)S(1)}, f16[16,6144]{1,0:T(8,128)(2,1)S(1)}, u32[]{:S(2)}, u32[]{:S(2)}) %collective-permute-start.19) | collective-permute-done | bytes 196640 | tf_op jit(solution)/shard_map/ppermute | solution.py:59
  71.4 0.1 fusion.5.sum_ref
  71.5 1.1 %shard_map.87 = f32[16,6144]{1,0:T(8,128)} custom-call(f32[16,6144]{1,0:T(8,128)S(1)} %fusion.5.sum_ref, f32[256,1]{1,0:T(8,128)S(1)} %get-tuple-element.49.unit_ref, f32[16,6144]{1,0:T(8,128)S(1)} %get-tuple-element.57.own_ref, f32[16,1]{1,0:T(8,128)S(1)} %get-tuple-element.58.rstd_ref, f32[1,6144]{1,0:T(1,128)S(1)} %bitcast.4, bf16[16,6144]{1,0:T(8,128)(2,1)S(1)} %copy-done), custom_call_target="tpu_custom_call" | custom-call | flops 1966080 | bytes 983040 | tf_op jit(solution)/shard_map/pallas_call | solution.py:324
  (26 shorter events, 0.2 us)
Async XLA Ops:
  1.0 14.1 %collective-permute-start.2 = (bf16[16,6144]{1,0:T(8,128)(2,1)S(1)}, bf16[16,6144]{1,0:T(8,128)(2,1)S(1)}, u32[]{:S(2)}, u32[]{:S(2)}) collective-permute-start(bf16[16,6144]{1,0:T(8,128)(2,1)S(1)} %multiply_convert_fusion), channel_id=1, source_target_pairs={{0,12},{1,13},{2,14},{3,15},{4,8},{5,9},{6,10},{7,11},{8,4},{9,5},... | collective-permute-start | bytes 589832 | tf_op jit(solution)/shard_map/ppermute | solution.py:59
  6.1 13.2 %collective-permute-start.1 = (bf16[16,6144]{1,0:T(8,128)(2,1)S(1)}, bf16[16,6144]{1,0:T(8,128)(2,1)S(1)}, u32[]{:S(2)}, u32[]{:S(2)}) collective-permute-start(bf16[16,6144]{1,0:T(8,128)(2,1)S(1)} %multiply_convert_fusion), channel_id=1, source_target_pairs={{0,4},{1,5},{2,6},{3,7},{4,0},{5,1},{6,2},{7,3},{8,12},{9,13},{10,... | collective-permute-start | bytes 589832 | tf_op jit(solution)/shard_map/ppermute | solution.py:59
  6.1 11.1 %copy-start.2 = (bf16[1536]{0:T(1024)(128)(2,1)S(1)}, bf16[1536]{0:T(1024)(128)(2,1)}, u32[]{:S(2)}) copy-start(bf16[1536]{0:T(1024)(128)(2,1)} %param.13) | copy-start | bytes 9220
  15.1 7.9 %collective-permute-start.3 = (bf16[16,6144]{1,0:T(8,128)(2,1)S(1)}, bf16[16,6144]{1,0:T(8,128)(2,1)S(1)}, u32[]{:S(2)}, u32[]{:S(2)}) collective-permute-start(bf16[16,6144]{1,0:T(8,128)(2,1)S(1)} %collective-permute-done.2), channel_id=1, source_target_pairs={{0,2},{1,3},{2,0},{3,1},{4,6},{5,7},{6,4},{7,5},{8,10},{9,11},{10,... | collective-permute-start | bytes 589832 | tf_op jit(solution)/shard_map/ppermute | solution.py:59
  16.7 10.5 %collective-permute-start = (bf16[16,6144]{1,0:T(8,128)(2,1)S(1)}, bf16[16,6144]{1,0:T(8,128)(2,1)S(1)}, u32[]{:S(2)}, u32[]{:S(2)}) collective-permute-start(bf16[16,6144]{1,0:T(8,128)(2,1)S(1)} %multiply_convert_fusion), channel_id=1, source_target_pairs={{0,2},{1,3},{2,0},{3,1},{4,6},{5,7},{6,4},{7,5},{8,10},{9,11},{10,... | collective-permute-start | bytes 589832 | tf_op jit(solution)/shard_map/ppermute | solution.py:59
  17.2 14.6 %collective-permute-start.5 = (bf16[16,6144]{1,0:T(8,128)(2,1)S(1)}, bf16[16,6144]{1,0:T(8,128)(2,1)S(1)}, u32[]{:S(2)}, u32[]{:S(2)}) collective-permute-start(bf16[16,6144]{1,0:T(8,128)(2,1)S(1)} %collective-permute-done.2), channel_id=1, source_target_pairs={{0,4},{1,5},{2,6},{3,7},{4,0},{5,1},{6,2},{7,3},{8,12},{9,13},{10,... | collective-permute-start | bytes 589832 | tf_op jit(solution)/shard_map/ppermute | solution.py:59
  23.0 8.7 %collective-permute-start.6 = (bf16[16,6144]{1,0:T(8,128)(2,1)S(1)}, bf16[16,6144]{1,0:T(8,128)(2,1)S(1)}, u32[]{:S(2)}, u32[]{:S(2)}) collective-permute-start(bf16[16,6144]{1,0:T(8,128)(2,1)S(1)} %collective-permute-done.3), channel_id=1, source_target_pairs={{0,4},{1,5},{2,6},{3,7},{4,0},{5,1},{6,2},{7,3},{8,12},{9,13},{10,... | collective-permute-start | bytes 589832 | tf_op jit(solution)/shard_map/ppermute | solution.py:59
  25.0 6.1 %collective-permute-start.4 = (bf16[16,6144]{1,0:T(8,128)(2,1)S(1)}, bf16[16,6144]{1,0:T(8,128)(2,1)S(1)}, u32[]{:S(2)}, u32[]{:S(2)}) collective-permute-start(bf16[16,6144]{1,0:T(8,128)(2,1)S(1)} %collective-permute-done.1), channel_id=1, source_target_pairs={{0,2},{1,3},{2,0},{3,1},{4,6},{5,7},{6,4},{7,5},{8,10},{9,11},{10,... | collective-permute-start | bytes 589832 | tf_op jit(solution)/shard_map/ppermute | solution.py:59
  27.2 7.2 %collective-permute-start.7 = (bf16[32,6144]{1,0:T(8,128)(2,1)S(1)}, bf16[32,6144]{1,0:T(8,128)(2,1)S(1)}, u32[]{:S(2)}, u32[]{:S(2)}) collective-permute-start(bf16[32,6144]{1,0:T(8,128)(2,1)S(1)} %pad_maximum_fusion.4), channel_id=1, source_target_pairs={{0,1},{1,0},{2,3},{3,2},{4,5},{5,4},{6,7},{7,6},{8,9},{9,8},{10,11... | collective-permute-start | bytes 1179656 | tf_op jit(solution)/shard_map/ppermute | solution.py:59
  31.1 3.3 %collective-permute-start.9 = (bf16[16,6144]{1,0:T(8,128)(2,1)S(1)}, bf16[16,6144]{1,0:T(8,128)(2,1)S(1)}, u32[]{:S(2)}, u32[]{:S(2)}) collective-permute-start(bf16[16,6144]{1,0:T(8,128)(2,1)S(1)} %collective-permute-done.4), channel_id=1, source_target_pairs={{0,1},{1,0},{2,3},{3,2},{4,5},{5,4},{6,7},{7,6},{8,9},{9,8},{10,11... | collective-permute-start | bytes 589832 | tf_op jit(solution)/shard_map/ppermute | solution.py:59
  31.7 2.7 %collective-permute-start.11 = (bf16[16,6144]{1,0:T(8,128)(2,1)S(1)}, bf16[16,6144]{1,0:T(8,128)(2,1)S(1)}, u32[]{:S(2)}, u32[]{:S(2)}) collective-permute-start(bf16[16,6144]{1,0:T(8,128)(2,1)S(1)} %collective-permute-done.6), channel_id=1, source_target_pairs={{0,1},{1,0},{2,3},{3,2},{4,5},{5,4},{6,7},{7,6},{8,9},{9,8},{10,11... | collective-permute-start | bytes 589832 | tf_op jit(solution)/shard_map/ppermute | solution.py:59
  31.9 1.8 %collective-permute-start.10 = (bf16[32,6144]{1,0:T(8,128)(2,1)S(1)}, bf16[32,6144]{1,0:T(8,128)(2,1)S(1)}, u32[]{:S(2)}, u32[]{:S(2)}) collective-permute-start(bf16[32,6144]{1,0:T(8,128)(2,1)S(1)} %get-tuple-element.71), channel_id=1, source_target_pairs={{0,1},{1,0},{2,3},{3,2},{4,5},{5,4},{6,7},{7,6},{8,9},{9,8},{10,11... | collective-permute-start | bytes 1179656 | tf_op jit(solution)/shard_map/ppermute | solution.py:59
  32.4 1.9 %collective-permute-start.8 = (bf16[32,6144]{1,0:T(8,128)(2,1)S(1)}, bf16[32,6144]{1,0:T(8,128)(2,1)S(1)}, u32[]{:S(2)}, u32[]{:S(2)}) collective-permute-start(bf16[32,6144]{1,0:T(8,128)(2,1)S(1)} %get-tuple-element.73), channel_id=1, source_target_pairs={{0,1},{1,0},{2,3},{3,2},{4,5},{5,4},{6,7},{7,6},{8,9},{9,8},{10,11... | collective-permute-start | bytes 1179656 | tf_op jit(solution)/shard_map/ppermute | solution.py:59
  46.2 2.4 %collective-permute-start.13 = (f16[64,6144]{1,0:T(8,128)(2,1)S(1)}, f16[64,6144]{1,0:T(8,128)(2,1)S(1)}, u32[]{:S(2)}, u32[]{:S(2)}) collective-permute-start(f16[64,6144]{1,0:T(8,128)(2,1)S(1)} %convert_element_type.56), channel_id=1, source_target_pairs={{0,1},{1,0},{2,3},{3,2},{4,5},{5,4},{6,7},{7,6},{8,9},{9,8},{10,11... | collective-permute-start | bytes 2359304 | tf_op jit(solution)/shard_map/ppermute | solution.py:59
  46.7 4.3 %collective-permute-start.12 = (f16[64,6144]{1,0:T(8,128)(2,1)S(1)}, f16[64,6144]{1,0:T(8,128)(2,1)S(1)}, u32[]{:S(2)}, u32[]{:S(2)}) collective-permute-start(f16[64,6144]{1,0:T(8,128)(2,1)S(1)} %convert_element_type.54), channel_id=1, source_target_pairs={{0,1},{1,0},{2,3},{3,2},{4,5},{5,4},{6,7},{7,6},{8,9},{9,8},{10,11... | collective-permute-start | bytes 2359304 | tf_op jit(solution)/shard_map/ppermute | solution.py:59
  48.8 7.9 %collective-permute-start.14 = (f16[16,6144]{1,0:T(8,128)(2,1)S(1)}, f16[16,6144]{1,0:T(8,128)(2,1)S(1)}, u32[]{:S(2)}, u32[]{:S(2)}) collective-permute-start(f16[16,6144]{1,0:T(8,128)(2,1)S(1)} %get-tuple-element.65), channel_id=1, source_target_pairs={{0,4},{1,5},{2,6},{3,7},{4,0},{5,1},{6,2},{7,3},{8,12},{9,13},{10,... | collective-permute-start | bytes 589832 | tf_op jit(solution)/shard_map/ppermute | solution.py:59
  50.9 9.6 %collective-permute-start.18 = (f16[16,6144]{1,0:T(8,128)(2,1)S(1)}, f16[16,6144]{1,0:T(8,128)(2,1)S(1)}, u32[]{:S(2)}, u32[]{:S(2)}) collective-permute-start(f16[16,6144]{1,0:T(8,128)(2,1)S(1)} %get-tuple-element.66), channel_id=1, source_target_pairs={{0,4},{1,5},{2,6},{3,7},{4,0},{5,1},{6,2},{7,3},{8,12},{9,13},{10,... | collective-permute-start | bytes 589832 | tf_op jit(solution)/shard_map/ppermute | solution.py:59
  51.3 7.0 %collective-permute-start.17 = (f16[16,6144]{1,0:T(8,128)(2,1)S(1)}, f16[16,6144]{1,0:T(8,128)(2,1)S(1)}, u32[]{:S(2)}, u32[]{:S(2)}) collective-permute-start(f16[16,6144]{1,0:T(8,128)(2,1)S(1)} %get-tuple-element.64), channel_id=1, source_target_pairs={{0,2},{1,3},{2,0},{3,1},{4,6},{5,7},{6,4},{7,5},{8,10},{9,11},{10,... | collective-permute-start | bytes 589832 | tf_op jit(solution)/shard_map/ppermute | solution.py:59
  56.7 6.3 %collective-permute-start.15 = (f16[16,6144]{1,0:T(8,128)(2,1)S(1)}, f16[16,6144]{1,0:T(8,128)(2,1)S(1)}, u32[]{:S(2)}, u32[]{:S(2)}) collective-permute-start(f16[16,6144]{1,0:T(8,128)(2,1)S(1)} %fusion.3), channel_id=1, source_target_pairs={{0,2},{1,3},{2,0},{3,1},{4,6},{5,7},{6,4},{7,5},{8,10},{9,11},{10,... | collective-permute-start | bytes 589832 | tf_op jit(solution)/shard_map/ppermute | solution.py:59
  58.3 13.2 %copy-start = (bf16[16,6144]{1,0:T(8,128)(2,1)S(1)}, bf16[16,6144]{1,0:T(8,128)(2,1)}, u32[]{:S(2)}) copy-start(bf16[16,6144]{1,0:T(8,128)(2,1)} %adjoint_ref.1) | copy-start | bytes 589828
  58.3 13.2 %copy-start.1 = (f32[6144]{0:T(1024)S(1)}, f32[6144]{0:T(1024)}, u32[]{:S(2)}) copy-start(f32[6144]{0:T(1024)} %param.11) | copy-start | bytes 73732
  60.6 10.8 %collective-permute-start.19 = (f16[16,6144]{1,0:T(8,128)(2,1)S(1)}, f16[16,6144]{1,0:T(8,128)(2,1)S(1)}, u32[]{:S(2)}, u32[]{:S(2)}) collective-permute-start(f16[16,6144]{1,0:T(8,128)(2,1)S(1)} %fusion.2), channel_id=1, source_target_pairs={{0,4},{1,5},{2,6},{3,7},{4,0},{5,1},{6,2},{7,3},{8,12},{9,13},{10,... | collective-permute-start | bytes 589832 | tf_op jit(solution)/shard_map/ppermute | solution.py:59
  63.2 8.2 %collective-permute-start.20 = (f16[16,6144]{1,0:T(8,128)(2,1)S(1)}, f16[16,6144]{1,0:T(8,128)(2,1)S(1)}, u32[]{:S(2)}, u32[]{:S(2)}) collective-permute-start(f16[16,6144]{1,0:T(8,128)(2,1)S(1)} %fusion.1), channel_id=1, source_target_pairs={{0,12},{1,13},{2,14},{3,15},{4,8},{5,9},{6,10},{7,11},{8,4},{9,5},... | collective-permute-start | bytes 589832 | tf_op jit(solution)/shard_map/ppermute | solution.py:59
  63.6 7.8 %collective-permute-start.16 = (f16[16,6144]{1,0:T(8,128)(2,1)S(1)}, f16[16,6144]{1,0:T(8,128)(2,1)S(1)}, u32[]{:S(2)}, u32[]{:S(2)}) collective-permute-start(f16[16,6144]{1,0:T(8,128)(2,1)S(1)} %get-tuple-element.55), channel_id=1, source_target_pairs={{0,2},{1,3},{2,0},{3,1},{4,6},{5,7},{6,4},{7,5},{8,10},{9,11},{10,... | collective-permute-start | bytes 589832 | tf_op jit(solution)/shard_map/ppermute | solution.py:59

commit v4 on v3

--- a/solution.py
+++ b/solution.py
@@ -86,7 +86,7 @@
         y3 = send(half(p31 + wide(z21)), SIDE)
         z20 = send(half(p20), PAIR)
         z3 = send(half(p30 + wide(y3) + wide(z20)), CROSS)
-        z1 = send(after(half(p10 + wide(y1)), z20), PAIR)
+        z1 = send(after(half(p10 + wide(y1)), z21), PAIR)
         y0 = send(after(half(p01), y3), SIDE)
         sums.append(p00 + wide(y0) + wide(z1) + wide(z3))
     return sums
@@ -148,46 +148,44 @@
     return product if acc is None else acc + product
 
 
-def first_kernel(rows, me_ref, latent_ref, shift_ref, scale_ref, wu_ref, wd_ref, h_ref, own_ref, rstd_ref, u_ref, next_ref, wd_out, latent_buf, shift_buf, scale_buf, w_buf, sems, w_sems, out_sems):
+def first_kernel(rows, me_ref, latent_ref, shift_ref, scale_ref, wu_ref, wd_ref, h_ref, own_ref, rstd_ref, wu_out, wd_out, latent_buf, shift_buf, scale_buf, sems, out_sems):
     copies = [
         load(source, target, sems.at[k])
         for k, (source, target) in enumerate([(latent_ref, latent_buf), (shift_ref, shift_buf), (scale_ref, scale_buf)])
     ]
-    n = w_buf.shape[1]
-    w_copies = load_parts(wu_ref, 0, w_buf, w_sems)
     outs = [
-        load(wu_ref.at[pl.ds(2 * n, n)], next_ref, out_sems.at[0]),
-        load(wd_ref.at[pl.ds(0, wd_out.shape[0])], wd_out, out_sems.at[1]),
+        load(source.at[pl.ds(0, out.shape[0])], out, out_sems.at[k])
+        for k, (source, out) in enumerate([(wu_ref, wu_out), (wd_ref, wd_out)])
     ]
     for copy in copies:
         copy.wait()
     normalize_rows(rows, me_ref, latent_buf, shift_buf, scale_buf, h_ref, own_ref, rstd_ref)
-    u = None
-    for k, copy in enumerate(w_copies):
-        copy.wait()
-        u = add_product(u, k * n, h_ref, w_buf[k])
-    u_ref[...] = u
     for copy in outs:
         copy.wait()
 
 
-def second_kernel(start, h_ref, u_ref, w_ref, wu_ref, u_out, next_ref, w_buf, sems):
-    n = w_buf.shape[0]
-    copy = load(wu_ref.at[pl.ds(start + n, n)], w_buf, sems.at[0])
-    ahead = load(wu_ref.at[pl.ds(start + 2 * n, n)], next_ref, sems.at[1])
-    u = add_product(u_ref[...], start, h_ref, w_ref[...])
+def second_kernel(h_ref, w_ref, wu_ref, wd_ref, u_out, next_ref, wd_out, w_buf, sems):
+    early, n = w_ref.shape[0], w_buf.shape[0]
+    copy = load(wu_ref.at[pl.ds(early, n)], w_buf, sems.at[0])
+    ahead = load(wu_ref.at[pl.ds(early + n, n)], next_ref, sems.at[1])
+    wd_copy = load(wd_ref.at[pl.ds(wd_out.shape[0], wd_out.shape[0])], wd_out, sems.at[2])
+    u = add_product(None, 0, h_ref, w_ref[...])
     copy.wait()
-    u_out[...] = add_product(u, start + n, h_ref, w_buf[...])
+    u_out[...] = add_product(u, early, h_ref, w_buf[...])
     ahead.wait()
-
-
-def third_kernel(start, h_ref, u_ref, w_ref, b_ref, wu_ref, wd_ref, slope_out, wd_out, w_buf, sems):
-    n = w_buf.shape[0]
-    copy = load(wu_ref.at[pl.ds(start + n, n)], w_buf, sems.at[0])
-    ahead = load(wd_ref.at[pl.ds(wd_out.shape[0], wd_out.shape[0])], wd_out, sems.at[1])
-    u = add_product(u_ref[...], start, h_ref, w_ref[...])
-    copy.wait()
-    slope_out[...] = add_product(u, start + n, h_ref, w_buf[...])
+    wd_copy.wait()
+
+
+def third_kernel(h_ref, u_ref, w_ref, b_ref, wu_ref, wd_ref, slope_out, wd_out, w_buf, w_sems, wd_sem):
+    parts, n, _ = w_buf.shape
+    start = wu_ref.shape[0] - parts * n
+    copies = load_parts(wu_ref, start, w_buf, w_sems)
+    ahead = load(wd_ref.at[pl.ds(2 * wd_out.shape[0], wd_out.shape[0])], wd_out, wd_sem)
+    u = add_product(u_ref[...], start - n, h_ref, w_ref[...])
+    for k, copy in enumerate(copies):
+        copy.wait()
+        u = add_product(u, start + k * n, h_ref, w_buf[k])
+    slope_out[...] = u
     width = slope_out.shape[1] // 3
     for j in range(3):
         cut = slice(j * width, (j + 1) * width)
@@ -196,46 +194,32 @@
 
 
 def du_kernel(*refs):
-    pieces, (wd0_ref, wd1_ref, slope_ref, wd_ref, wu_ref, du_ref, unit_ref, wu_out, wd_buf, sems) = refs[:6], refs[6:]
-    width, at = wd_buf.shape[0], 0
-    wd_copy = load(wd_ref.at[pl.ds(2 * width, width)], wd_buf, sems.at[0])
-    wu_copy = load(wu_ref.at[pl.ds(0, wu_out.shape[0])], wu_out, sems.at[1])
+    pieces, wds, (slope_ref, wu_ref, du_ref, unit_ref, wu_out, sem) = refs[:6], refs[6:9], refs[9:]
+    wu_copy = load(wu_ref.at[pl.ds(0, wu_out.shape[0])], wu_out, sem)
+    at = 0
     for piece in pieces:
         top = jnp.max(jnp.abs(piece[...].astype(jnp.float32)), axis=1, keepdims=True)
         unit_ref[at : at + piece.shape[0], :] = 16.0 * jnp.maximum(top, 1e-30)
         at += piece.shape[0]
     gated = jnp.concatenate([piece[...] for piece in pieces], axis=0)
-    for k, wd in enumerate((wd0_ref, wd1_ref, wd_buf)):
-        if k == 2:
-            wd_copy.wait()
-        cut = slice(k * width, (k + 1) * width)
+    for k, wd in enumerate(wds):
+        cut = slice(k * wd.shape[0], (k + 1) * wd.shape[0])
         du_ref[:, cut] = (rows_t(gated, wd[...]) * slope_ref[:, cut]).astype(du_ref.dtype)
     wu_copy.wait()
 
 
-def dh_kernel(start, ahead, du_ref, unit_ref, early_ref, wu_ref, *refs):
-    outs, refs = refs[:4], refs[4:]
-    if ahead:
-        ahead_out, w_buf, sems, ahead_sem = refs
-    else:
-        w_buf, sems = refs
-    n, early, width = outs[0].shape[0], early_ref.shape[0], w_buf.shape[1]
-    copies = load_parts(wu_ref, start + early, w_buf, sems)
-    if ahead:
-        ahead_copy = load(wu_ref.at[pl.ds(start + outs[0].shape[1], ahead)], ahead_out, ahead_sem)
+def dh_kernel(width, du_ref, unit_ref, early_ref, wu_ref, *refs):
+    outs, (w_buf, sem) = refs[:-2], refs[-2:]
+    n, early = outs[0].shape[0], early_ref.shape[0]
+    copy = load(wu_ref.at[pl.ds(early, w_buf.shape[0])], w_buf, sem)
     scale = 1.0 / unit_ref[...]
-    for at in range(0, outs[0].shape[1], width):
-        if at < early:
-            w = early_ref[at : at + width, :]
-        else:
-            k = (at - early) // width
-            copies[k].wait()
-            w = w_buf[k]
+    for at in range(0, wu_ref.shape[0], width):
+        if at == early:
+            copy.wait()
+        w = early_ref[at : at + width, :] if at < early else w_buf[at - early : at - early + width, :]
         dh = rows_t(du_ref[...], w) * scale
         for j, out in enumerate(outs):
             out[:, at : at + width] = dh[j * n : (j + 1) * n]
-    if ahead:
-        ahead_copy.wait()
 
 
 def finish_kernel(sum_ref, unit_ref, own_ref, rstd_ref, scale_ref, adjoint_ref, out_ref):
@@ -266,59 +250,58 @@
     depth, third = d // 6, ff // 3
     wd_shape = shape((third, d), bf16)
     u_shape, part_shape = shape((tokens, ff), f32), shape((depth, ff), bf16)
-    part = pltpu.VMEM((depth, ff), bf16)
     sems = lambda n: pltpu.SemaphoreType.DMA((n,))
-    h, own_normed, own_rstd, u, part2, wd0 = kernel(
+    h, own_normed, own_rstd, wu_early, wd0 = kernel(
         functools.partial(first_kernel, rows),
         [SMEM] + [HBM] * 5,
-        [shape((tokens, d), bf16), shape((rows, d), f32), shape((rows, 1), f32), u_shape, part_shape, wd_shape],
-        work // 2, 2 * d * ff, 18,
-        scratch_shapes=[pltpu.VMEM((tokens, d), bf16), pltpu.VMEM((1, d), f32), pltpu.VMEM((1, d), f32)]
-        + [pltpu.VMEM((2, depth, ff), bf16), sems(3), sems(2), sems(2)],
+        [shape((tokens, d), bf16), shape((rows, d), f32), shape((rows, 1), f32), shape((2 * depth, ff), bf16), wd_shape],
+        work // 2, 2 * d * ff, 16,
+        scratch_shapes=[pltpu.VMEM((tokens, d), bf16), pltpu.VMEM((1, d), f32), pltpu.VMEM((1, d), f32), sems(3), sems(2)],
     )(me.reshape(1).astype(jnp.int32), stay(latent), stay(shift_row[None]), stay(scale), w_up, w_down)
 
-    b10, b30 = after(b10, u), after(b30, u)
+    cat = lambda *blocks: jnp.concatenate(blocks, axis=0)
+    b01, b30, b10, _ = lax.optimization_barrier((b01, b30, b10, h))
     b31 = send(b30, SIDE)
     b20 = send(b30, PAIR)
-    u, part4 = kernel(
-        functools.partial(second_kernel, 2 * depth),
-        [VMEM] * 3 + [HBM],
-        [u_shape, part_shape],
+    c0, c13 = send(cat(b00, b01), CORE), send(cat(b10, b30), CORE)
+    u, part, wd1 = kernel(
+        second_kernel,
+        [VMEM] * 2 + [HBM] * 2,
+        [u_shape, part_shape, wd_shape],
         work // 3, d * ff, 12,
-        scratch_shapes=[part, sems(2)],
-    )(h, after(u, b30), part2, w_up)
+        scratch_shapes=[pltpu.VMEM((depth, ff), bf16), sems(3)],
+    )(after(h, b30), wu_early, w_up, w_down)
 
     b31 = after(b31, u)
     b21 = send(b31, PAIR)
     b11 = send(after(b10, b31), SIDE)
-    slope, wd1 = kernel(
-        functools.partial(third_kernel, 4 * depth),
+    c32 = send(cat(b31, b20), CORE)
+    slope, wd2 = kernel(
+        third_kernel,
         [VMEM] * 4 + [HBM] * 2,
         [u_shape, wd_shape],
         work // 3, d * ff, 12,
-        scratch_shapes=[part, sems(2)],
-    )(h, after(u, b31), part4, b_up[None], w_up, w_down)
+        scratch_shapes=[pltpu.VMEM((2, depth, ff), bf16), sems(2), pltpu.SemaphoreType.DMA],
+    )(h, after(u, b31, b20, c0, c13), part, b_up[None], w_up, w_down)
 
     b11, b21 = after(b11, slope), after(b21, slope)
-    cat = lambda *blocks: jnp.concatenate(blocks, axis=0)
-    c0, c13, c32 = [send(cat(*x), CORE) for x in ((b00, b01), (b10, b30), (b31, b20))]
     c11, c21 = send(b11, CORE), send(b21, CORE)
     pieces = [cat(b00, b01, b10, b11), cat(b30, b31), cat(b20, b21)]
     pieces += [cat(c0, c13[:rows], c11), cat(c13[rows:], c32[:rows]), cat(c32[rows:], c21)]
-    early = 2 * depth
+    early = 4 * depth
     du, unit, wu_early = kernel(
         du_kernel,
-        [VMEM] * 9 + [HBM] * 2,
+        [VMEM] * 10 + [HBM],
         [shape((tokens, ff), bf16), shape((tokens, 1), f32), shape((early, ff), bf16)],
-        work, 2 * d * ff, 16,
-        scratch_shapes=[pltpu.VMEM((third, d), bf16), sems(2)],
-    )(*pieces, wd0, wd1, slope, w_down, w_up)
+        work, 2 * d * ff, 10,
+        scratch_shapes=[pltpu.SemaphoreType.DMA],
+    )(*pieces, wd0, wd1, wd2, slope, w_up)
     quarters = kernel(
-        functools.partial(dh_kernel, 0, 0),
+        functools.partial(dh_kernel, depth),
         [VMEM] * 3 + [HBM],
         [shape((tokens // 4, d), f32)] * 4,
-        work, 2 * d * ff, 20,
-        scratch_shapes=[pltpu.VMEM((4, depth, ff), bf16), pltpu.SemaphoreType.DMA((4,))],
+        work, 2 * d * ff, 12,
+        scratch_shapes=[pltpu.VMEM((2 * depth, ff), bf16), pltpu.SemaphoreType.DMA],
     )(du, unit, wu_early, w_up)
     (total,) = scatter_sums([quarters], rows)
     return kernel(

time: 72.7 us -> 69.1 us (0.950)
  starting transfers between devices: 23.9 us -> 19.5 us
    ppermute x21, starting transfers between devices: 23.9 us -> 19.5 us  [send(): return lax.ppermute(x, 'fsdp', pairs)]
    pallas_call x4, Pallas kernels: 18.3 us -> 20.2 us  [the longest x1 5.47 us: line_of_four(): kernel(functools.partial(dh_kernel, depth), [VMEM] * 3 + [HBM], [shape((t...]
    pallas_call x1, Pallas kernels: 8.97 us -> 7.11 us  [line_of_four(): kernel(functools.partial(first_kernel, rows), [SMEM] + [HBM] * 5, [shape(...]
  transfers between devices with their start and end apart: 21 -> 21, of which waited for: 9 -> 10; matrix products, arithmetic and copies ran while one was open for 2% -> 2% of each run, Pallas kernels for 22% -> 24%
where the time goes in v4:
time: 69.1 us; the launch traced here: 69 us
  Pallas kernels  28.4 us (41%)
  starting transfers between devices  19.5 us (28%)
  waiting for transfers between devices  18.4 us (27%)
  other arithmetic  2.2 us (3%)
    ppermute x21, starting transfers between devices, send(): return lax.ppermute(x, 'fsdp', pairs)  19.5 us
    ppermute x21, waiting for transfers between devices, send(): return lax.ppermute(x, 'fsdp', pairs)  18.4 us
    pallas_call x1, Pallas kernels, line_of_four(): kernel(functools.partial(first_kernel, rows), [SMEM] + [HBM] * 5, [shape(...  7.11 us
    pallas_call x1, Pallas kernels, line_of_four(): kernel(functools.partial(dh_kernel, depth), [VMEM] * 3 + [HBM], [shape((t...  5.47 us
    pallas_call x1, Pallas kernels, line_of_four(): kernel(du_kernel, [VMEM] * 10 + [HBM], [shape((tokens, ff), bf16), shape(...  5.23 us
    pallas_call x1, Pallas kernels, line_of_four(): kernel(second_kernel, [VMEM] * 2 + [HBM] * 2, [u_shape, part_shape, wd_sh...  4.76 us
    pallas_call x1, Pallas kernels, line_of_four(): kernel(third_kernel, [VMEM] * 4 + [HBM] * 2, [u_shape, wd_shape], work //...  4.69 us
  transfers between devices with their start and end apart: 21, of which 10 were waited for; matrix products, arithmetic and copies ran while one was open for 2% of the time, Pallas kernels for 24%

profile of v4, /device:TPU:0, one launch (start us, length us, event | category | flops | bytes accessed | tf_op | source)
XLA Modules:
  0.0 69.0 jit_solution(7817774109938685611)
XLA Ops:
  0.0 1.0 %multiply_convert_fusion = bf16[16,6144]{1,0:T(8,128)(2,1)S(1)} fusion(bf16[16,6144]{1,0:T(8,128)(2,1)} %adjoint_ref.1, f32[6144]{0:T(1024)} %param.12), kind=kLoop, calls=%fused_computation.21 | loop fusion | flops 294912 | bytes 417792 | tf_op jit(solution)/shard_map/convert_element_type | solution.py:245
  1.0 3.1 %collective-permute-start.2 = (bf16[16,6144]{1,0:T(8,128)(2,1)S(1)}, bf16[16,6144]{1,0:T(8,128)(2,1)S(1)}, u32[]{:S(2)}, u32[]{:S(2)}) collective-permute-start(bf16[16,6144]{1,0:T(8,128)(2,1)S(1)} %multiply_convert_fusion), channel_id=1, source_target_pairs={{0,4},{1,5},{2,6},{3,7},{4,0},{5,1},{6,2},{7,3},{8,12},{9,13},{10,... | collective-permute-start | bytes 589832 | tf_op jit(solution)/shard_map/ppermute | solution.py:59
  4.1 2.5 %collective-permute-start.1 = (bf16[16,6144]{1,0:T(8,128)(2,1)S(1)}, bf16[16,6144]{1,0:T(8,128)(2,1)S(1)}, u32[]{:S(2)}, u32[]{:S(2)}) collective-permute-start(bf16[16,6144]{1,0:T(8,128)(2,1)S(1)} %multiply_convert_fusion), channel_id=1, source_target_pairs={{0,12},{1,13},{2,14},{3,15},{4,8},{5,9},{6,10},{7,11},{8,4},{9,5},... | collective-permute-start | bytes 589832 | tf_op jit(solution)/shard_map/ppermute | solution.py:59
  6.5 1.5 %collective-permute-start = (bf16[16,6144]{1,0:T(8,128)(2,1)S(1)}, bf16[16,6144]{1,0:T(8,128)(2,1)S(1)}, u32[]{:S(2)}, u32[]{:S(2)}) collective-permute-start(bf16[16,6144]{1,0:T(8,128)(2,1)S(1)} %multiply_convert_fusion), channel_id=1, source_target_pairs={{0,2},{1,3},{2,0},{3,1},{4,6},{5,7},{6,4},{7,5},{8,10},{9,11},{10,... | collective-permute-start | bytes 589832 | tf_op jit(solution)/shard_map/ppermute | solution.py:59
  8.1 7.1 %shard_map.82 = (bf16[256,6144]{1,0:T(8,128)(2,1)S(1)}, f32[16,6144]{1,0:T(8,128)S(1)}, f32[16,1]{1,0:T(8,128)S(1)}, bf16[2048,1536]{1,0:T(8,128)(2,1)S(1)}, bf16[512,6144]{1,0:T(8,128)(2,1)S(1)}) custom-call(s32[1]{0:T(128)} %bitcast.me_ref, bf16[256,6144]{1,0:T(8,128)(2,1)} %latent_ref.1, f32[1,6144]{1,0:T(1,128)} %bitcast.5, f32[1,6144]{1,0:T(1,128)} %bitcast.3, ...), custom_call_target="tpu_custom_call" | custom-call | flops 2415919104 | bytes 18874368 | tf_op jit(solution)/shard_map/pallas_call | solution.py:254
  15.2 0.3 collective-permute-done.1
  15.5 0.6 collective-permute-start.5
  16.0 1.5 %collective-permute-start.3 = (bf16[16,6144]{1,0:T(8,128)(2,1)S(1)}, bf16[16,6144]{1,0:T(8,128)(2,1)S(1)}, u32[]{:S(2)}, u32[]{:S(2)}) collective-permute-start(bf16[16,6144]{1,0:T(8,128)(2,1)S(1)} %collective-permute-done.1), channel_id=1, source_target_pairs={{0,2},{1,3},{2,0},{3,1},{4,6},{5,7},{6,4},{7,5},{8,10},{9,11},{10,... | collective-permute-start | bytes 589832 | tf_op jit(solution)/shard_map/ppermute | solution.py:59
  17.6 0.1 collective-permute-start.6
  17.7 4.8 %shard_map.83 = (f32[256,1536]{1,0:T(8,128)S(1)}, bf16[1024,1536]{1,0:T(8,128)(2,1)S(1)}, bf16[512,6144]{1,0:T(8,128)(2,1)S(1)}) custom-call(bf16[256,6144]{1,0:T(8,128)(2,1)S(1)} %get-tuple-element.37.h_ref, bf16[2048,1536]{1,0:T(8,128)(2,1)S(1)} %get-tuple-element.38.w_ref, bf16[6144,1536]{1,0:T(8,128)(2,1)} %wu_ref.7, bf16[1536,6144]{1,0:T(8,128)(2,1)} %wd_ref.5), custom_call_target="tpu_custom_call" | custom-call | flops 1610612736 | bytes 9437184 | tf_op jit(solution)/shard_map/pallas_call | solution.py:267
  22.5 0.1 pad_maximum_fusion.6
  22.6 0.6 collective-permute-start.7
  23.1 1.5 %collective-permute-start.8 = (bf16[16,6144]{1,0:T(8,128)(2,1)S(1)}, bf16[16,6144]{1,0:T(8,128)(2,1)S(1)}, u32[]{:S(2)}, u32[]{:S(2)}) collective-permute-start(bf16[16,6144]{1,0:T(8,128)(2,1)S(1)} %collective-permute-done.3), channel_id=1, source_target_pairs={{0,4},{1,5},{2,6},{3,7},{4,0},{5,1},{6,2},{7,3},{8,12},{9,13},{10,... | collective-permute-start | bytes 589832 | tf_op jit(solution)/shard_map/ppermute | solution.py:59
  24.6 0.5 collective-permute-start.4
  25.1 0.1 collective-permute-start.10
  25.2 4.7 %shard_map.84 = (f32[256,1536]{1,0:T(8,128)S(1)}, bf16[512,6144]{1,0:T(8,128)(2,1)S(1)}) custom-call(bf16[256,6144]{1,0:T(8,128)(2,1)S(1)} %get-tuple-element.37.h_ref, f32[256,1536]{1,0:T(8,128)S(1)} %get-tuple-element.42.u_ref, bf16[1024,1536]{1,0:T(8,128)(2,1)S(1)} %get-tuple-element.43.w_ref, bf16[1,1536]{1,0:T(2,128)(2,1)S(1)} %broadcast_in_dim.12.b_ref, ...), custom_call_target="tpu_custom_call" | custom-call | flops 1610612736 | bytes 9437184 | tf_op jit(solution)/shard_map/pallas_call | solution.py:279
  29.9 0.1 collective-permute-done.8
  30.0 1.2 %collective-permute-done.4 = bf16[16,6144]{1,0:T(8,128)(2,1)S(1)} collective-permute-done((bf16[16,6144]{1,0:T(8,128)(2,1)S(1)}, bf16[16,6144]{1,0:T(8,128)(2,1)S(1)}, u32[]{:S(2)}, u32[]{:S(2)}) %collective-permute-start.4) | collective-permute-done | bytes 196640 | tf_op jit(solution)/shard_map/ppermute | solution.py:59
  31.2 0.5 collective-permute-start.11
  31.7 0.1 pad_maximum_fusion.refs_0_
  31.9 1.0 %collective-permute-done.11 = bf16[16,6144]{1,0:T(8,128)(2,1)S(1)} collective-permute-done((bf16[16,6144]{1,0:T(8,128)(2,1)S(1)}, bf16[16,6144]{1,0:T(8,128)(2,1)S(1)}, u32[]{:S(2)}, u32[]{:S(2)}) %collective-permute-start.11) | collective-permute-done | bytes 196640 | tf_op jit(solution)/shard_map/ppermute | solution.py:59
  32.9 0.1 pad_maximum_fusion.1.refs_3_
  33.0 5.2 %shard_map.85 = (bf16[256,1536]{1,0:T(8,128)(2,1)S(1)}, f32[256,1]{1,0:T(8,128)S(1)}, bf16[4096,1536]{1,0:T(8,128)(2,1)S(1)}) custom-call(bf16[64,6144]{1,0:T(8,128)(2,1)S(1)} %pad_maximum_fusion.refs_0_, bf16[32,6144]{1,0:T(8,128)(2,1)S(1)} %get-tuple-element.74.refs_1_, bf16[32,6144]{1,0:T(8,128)(2,1)S(1)} %pad_maximum_fusion.5.refs_2_, ...), custom_call_target="tpu_custom_call" | custom-call | flops 4831838208 | bytes 18874368 | tf_op jit(solution)/shard_map/pallas_call | solution.py:292
  38.2 5.5 %shard_map.86 = (f32[64,6144]{1,0:T(8,128)S(1)}, f32[64,6144]{1,0:T(8,128)S(1)}, f32[64,6144]{1,0:T(8,128)S(1)}, f32[64,6144]{1,0:T(8,128)S(1)}) custom-call(bf16[256,1536]{1,0:T(8,128)(2,1)S(1)} %get-tuple-element.50.du_ref, f32[256,1]{1,0:T(8,128)S(1)} %get-tuple-element.51.unit_ref, bf16[4096,1536]{1,0:T(8,128)(2,1)S(1)} %get-tuple-element.52.early_ref, ...), custom_call_target="tpu_custom_call" | custom-call | flops 4831838208 | bytes 18874368 | tf_op jit(solution)/shard_map/pallas_call | solution.py:299
  43.7 0.1 convert_element_type.56
  43.8 0.3 collective-permute-start.13
  44.1 0.1 convert_element_type.54
  44.2 0.3 collective-permute-start.12
  44.5 1.6 %collective-permute-done.13 = f16[64,6144]{1,0:T(8,128)(2,1)S(1)} collective-permute-done((f16[64,6144]{1,0:T(8,128)(2,1)S(1)}, f16[64,6144]{1,0:T(8,128)(2,1)S(1)}, u32[]{:S(2)}, u32[]{:S(2)}) %collective-permute-start.13) | collective-permute-done | bytes 786464 | tf_op jit(solution)/shard_map/ppermute | solution.py:59
  46.2 0.2 fusion.7
  46.4 0.1 fusion.9
  46.5 0.6 collective-permute-start.14
  47.1 1.5 %collective-permute-start.19 = (f16[16,6144]{1,0:T(8,128)(2,1)S(1)}, f16[16,6144]{1,0:T(8,128)(2,1)S(1)}, u32[]{:S(2)}, u32[]{:S(2)}) collective-permute-start(f16[16,6144]{1,0:T(8,128)(2,1)S(1)} %get-tuple-element.68), channel_id=1, source_target_pairs={{0,4},{1,5},{2,6},{3,7},{4,0},{5,1},{6,2},{7,3},{8,12},{9,13},{10,... | collective-permute-start | bytes 589832 | tf_op jit(solution)/shard_map/ppermute | solution.py:59
  48.6 0.3 fusion.6
  48.9 0.1 fusion.8
  48.9 0.8 %collective-permute-start.17 = (f16[16,6144]{1,0:T(8,128)(2,1)S(1)}, f16[16,6144]{1,0:T(8,128)(2,1)S(1)}, u32[]{:S(2)}, u32[]{:S(2)}) collective-permute-start(f16[16,6144]{1,0:T(8,128)(2,1)S(1)} %get-tuple-element.66), channel_id=1, source_target_pairs={{0,2},{1,3},{2,0},{3,1},{4,6},{5,7},{6,4},{7,5},{8,10},{9,11},{10,... | collective-permute-start | bytes 589832 | tf_op jit(solution)/shard_map/ppermute | solution.py:59
  49.7 4.6 %collective-permute-done.14 = f16[16,6144]{1,0:T(8,128)(2,1)S(1)} collective-permute-done((f16[16,6144]{1,0:T(8,128)(2,1)S(1)}, f16[16,6144]{1,0:T(8,128)(2,1)S(1)}, u32[]{:S(2)}, u32[]{:S(2)}) %collective-permute-start.14) | collective-permute-done | bytes 196640 | tf_op jit(solution)/shard_map/ppermute | solution.py:59
  54.3 0.8 %collective-permute-start.15 = (f16[16,6144]{1,0:T(8,128)(2,1)S(1)}, f16[16,6144]{1,0:T(8,128)(2,1)S(1)}, u32[]{:S(2)}, u32[]{:S(2)}) collective-permute-start(f16[16,6144]{1,0:T(8,128)(2,1)S(1)} %fusion.3), channel_id=1, source_target_pairs={{0,2},{1,3},{2,0},{3,1},{4,6},{5,7},{6,4},{7,5},{8,10},{9,11},{10,... | collective-permute-start | bytes 589832 | tf_op jit(solution)/shard_map/ppermute | solution.py:59
  55.1 0.4 collective-permute-done.17
  55.5 0.6 collective-permute-start.18
  56.2 2.3 %collective-permute-done.19 = f16[16,6144]{1,0:T(8,128)(2,1)S(1)} collective-permute-done((f16[16,6144]{1,0:T(8,128)(2,1)S(1)}, f16[16,6144]{1,0:T(8,128)(2,1)S(1)}, u32[]{:S(2)}, u32[]{:S(2)}) %collective-permute-start.19) | collective-permute-done | bytes 196640 | tf_op jit(solution)/shard_map/ppermute | solution.py:59
  58.5 1.6 %collective-permute-done.15 = f16[16,6144]{1,0:T(8,128)(2,1)S(1)} collective-permute-done((f16[16,6144]{1,0:T(8,128)(2,1)S(1)}, f16[16,6144]{1,0:T(8,128)(2,1)S(1)}, u32[]{:S(2)}, u32[]{:S(2)}) %collective-permute-start.15) | collective-permute-done | bytes 196640 | tf_op jit(solution)/shard_map/ppermute | solution.py:59
  60.1 0.1 fusion.1
  60.2 1.6 %collective-permute-start.20 = (f16[16,6144]{1,0:T(8,128)(2,1)S(1)}, f16[16,6144]{1,0:T(8,128)(2,1)S(1)}, u32[]{:S(2)}, u32[]{:S(2)}) collective-permute-start(f16[16,6144]{1,0:T(8,128)(2,1)S(1)} %fusion.1), channel_id=1, source_target_pairs={{0,12},{1,13},{2,14},{3,15},{4,8},{5,9},{6,10},{7,11},{8,4},{9,5},... | collective-permute-start | bytes 589832 | tf_op jit(solution)/shard_map/ppermute | solution.py:59
  61.8 0.6 collective-permute-start.16
  62.4 5.3 %collective-permute-done.20 = f16[16,6144]{1,0:T(8,128)(2,1)S(1)} collective-permute-done((f16[16,6144]{1,0:T(8,128)(2,1)S(1)}, f16[16,6144]{1,0:T(8,128)(2,1)S(1)}, u32[]{:S(2)}, u32[]{:S(2)}) %collective-permute-start.20) | collective-permute-done | bytes 196640 | tf_op jit(solution)/shard_map/ppermute | solution.py:59
  67.8 0.1 fusion.5.sum_ref
  67.9 1.1 %shard_map.87 = f32[16,6144]{1,0:T(8,128)} custom-call(f32[16,6144]{1,0:T(8,128)S(1)} %fusion.5.sum_ref, f32[256,1]{1,0:T(8,128)S(1)} %get-tuple-element.51.unit_ref, f32[16,6144]{1,0:T(8,128)S(1)} %get-tuple-element.59.own_ref, f32[16,1]{1,0:T(8,128)S(1)} %get-tuple-element.60.rstd_ref, f32[1,6144]{1,0:T(1,128)S(1)} %bitcast.4, bf16[16,6144]{1,0:T(8,128)(2,1)S(1)} %copy-done), custom_call_target="tpu_custom_call" | custom-call | flops 1966080 | bytes 983040 | tf_op jit(solution)/shard_map/pallas_call | solution.py:307
  (27 shorter events, 0.3 us)
Async XLA Ops:
  1.0 14.2 %collective-permute-start.2 = (bf16[16,6144]{1,0:T(8,128)(2,1)S(1)}, bf16[16,6144]{1,0:T(8,128)(2,1)S(1)}, u32[]{:S(2)}, u32[]{:S(2)}) collective-permute-start(bf16[16,6144]{1,0:T(8,128)(2,1)S(1)} %multiply_convert_fusion), channel_id=1, source_target_pairs={{0,4},{1,5},{2,6},{3,7},{4,0},{5,1},{6,2},{7,3},{8,12},{9,13},{10,... | collective-permute-start | bytes 589832 | tf_op jit(solution)/shard_map/ppermute | solution.py:59
  4.1 11.4 %collective-permute-start.1 = (bf16[16,6144]{1,0:T(8,128)(2,1)S(1)}, bf16[16,6144]{1,0:T(8,128)(2,1)S(1)}, u32[]{:S(2)}, u32[]{:S(2)}) collective-permute-start(bf16[16,6144]{1,0:T(8,128)(2,1)S(1)} %multiply_convert_fusion), channel_id=1, source_target_pairs={{0,12},{1,13},{2,14},{3,15},{4,8},{5,9},{6,10},{7,11},{8,4},{9,5},... | collective-permute-start | bytes 589832 | tf_op jit(solution)/shard_map/ppermute | solution.py:59
  6.5 8.9 %collective-permute-start = (bf16[16,6144]{1,0:T(8,128)(2,1)S(1)}, bf16[16,6144]{1,0:T(8,128)(2,1)S(1)}, u32[]{:S(2)}, u32[]{:S(2)}) collective-permute-start(bf16[16,6144]{1,0:T(8,128)(2,1)S(1)} %multiply_convert_fusion), channel_id=1, source_target_pairs={{0,2},{1,3},{2,0},{3,1},{4,6},{5,7},{6,4},{7,5},{8,10},{9,11},{10,... | collective-permute-start | bytes 589832 | tf_op jit(solution)/shard_map/ppermute | solution.py:59
  15.5 7.0 %collective-permute-start.5 = (bf16[16,6144]{1,0:T(8,128)(2,1)S(1)}, bf16[16,6144]{1,0:T(8,128)(2,1)S(1)}, u32[]{:S(2)}, u32[]{:S(2)}) collective-permute-start(bf16[16,6144]{1,0:T(8,128)(2,1)S(1)} %collective-permute-done.1), channel_id=1, source_target_pairs={{0,4},{1,5},{2,6},{3,7},{4,0},{5,1},{6,2},{7,3},{8,12},{9,13},{10,... | collective-permute-start | bytes 589832 | tf_op jit(solution)/shard_map/ppermute | solution.py:59
  16.0 6.4 %collective-permute-start.3 = (bf16[16,6144]{1,0:T(8,128)(2,1)S(1)}, bf16[16,6144]{1,0:T(8,128)(2,1)S(1)}, u32[]{:S(2)}, u32[]{:S(2)}) collective-permute-start(bf16[16,6144]{1,0:T(8,128)(2,1)S(1)} %collective-permute-done.1), channel_id=1, source_target_pairs={{0,2},{1,3},{2,0},{3,1},{4,6},{5,7},{6,4},{7,5},{8,10},{9,11},{10,... | collective-permute-start | bytes 589832 | tf_op jit(solution)/shard_map/ppermute | solution.py:59
  17.6 7.6 %collective-permute-start.6 = (bf16[32,6144]{1,0:T(8,128)(2,1)S(1)}, bf16[32,6144]{1,0:T(8,128)(2,1)S(1)}, u32[]{:S(2)}, u32[]{:S(2)}) collective-permute-start(bf16[32,6144]{1,0:T(8,128)(2,1)S(1)} %pad_maximum_fusion.2), channel_id=1, source_target_pairs={{0,1},{1,0},{2,3},{3,2},{4,5},{5,4},{6,7},{7,6},{8,9},{9,8},{10,11... | collective-permute-start | bytes 1179656 | tf_op jit(solution)/shard_map/ppermute | solution.py:59
  22.4 2.6 %copy-start.2 = (bf16[1536]{0:T(1024)(128)(2,1)S(1)}, bf16[1536]{0:T(1024)(128)(2,1)}, u32[]{:S(2)}) copy-start(bf16[1536]{0:T(1024)(128)(2,1)} %param.13) | copy-start | bytes 9220
  22.6 2.6 %collective-permute-start.7 = (bf16[32,6144]{1,0:T(8,128)(2,1)S(1)}, bf16[32,6144]{1,0:T(8,128)(2,1)S(1)}, u32[]{:S(2)}, u32[]{:S(2)}) collective-permute-start(bf16[32,6144]{1,0:T(8,128)(2,1)S(1)} %get-tuple-element.75), channel_id=1, source_target_pairs={{0,1},{1,0},{2,3},{3,2},{4,5},{5,4},{6,7},{7,6},{8,9},{9,8},{10,11... | collective-permute-start | bytes 1179656 | tf_op jit(solution)/shard_map/ppermute | solution.py:59
  23.1 6.9 %collective-permute-start.8 = (bf16[16,6144]{1,0:T(8,128)(2,1)S(1)}, bf16[16,6144]{1,0:T(8,128)(2,1)S(1)}, u32[]{:S(2)}, u32[]{:S(2)}) collective-permute-start(bf16[16,6144]{1,0:T(8,128)(2,1)S(1)} %collective-permute-done.3), channel_id=1, source_target_pairs={{0,4},{1,5},{2,6},{3,7},{4,0},{5,1},{6,2},{7,3},{8,12},{9,13},{10,... | collective-permute-start | bytes 589832 | tf_op jit(solution)/shard_map/ppermute | solution.py:59
  24.6 6.6 %collective-permute-start.4 = (bf16[16,6144]{1,0:T(8,128)(2,1)S(1)}, bf16[16,6144]{1,0:T(8,128)(2,1)S(1)}, u32[]{:S(2)}, u32[]{:S(2)}) collective-permute-start(bf16[16,6144]{1,0:T(8,128)(2,1)S(1)} %collective-permute-done.2), channel_id=1, source_target_pairs={{0,2},{1,3},{2,0},{3,1},{4,6},{5,7},{6,4},{7,5},{8,10},{9,11},{10,... | collective-permute-start | bytes 589832 | tf_op jit(solution)/shard_map/ppermute | solution.py:59
  25.1 6.7 %collective-permute-start.10 = (bf16[32,6144]{1,0:T(8,128)(2,1)S(1)}, bf16[32,6144]{1,0:T(8,128)(2,1)S(1)}, u32[]{:S(2)}, u32[]{:S(2)}) collective-permute-start(bf16[32,6144]{1,0:T(8,128)(2,1)S(1)} %get-tuple-element.73), channel_id=1, source_target_pairs={{0,1},{1,0},{2,3},{3,2},{4,5},{5,4},{6,7},{7,6},{8,9},{9,8},{10,11... | collective-permute-start | bytes 1179656 | tf_op jit(solution)/shard_map/ppermute | solution.py:59
  31.2 1.8 %collective-permute-start.9 = (bf16[16,6144]{1,0:T(8,128)(2,1)S(1)}, bf16[16,6144]{1,0:T(8,128)(2,1)S(1)}, u32[]{:S(2)}, u32[]{:S(2)}) collective-permute-start(bf16[16,6144]{1,0:T(8,128)(2,1)S(1)} %collective-permute-done.4), channel_id=1, source_target_pairs={{0,1},{1,0},{2,3},{3,2},{4,5},{5,4},{6,7},{7,6},{8,9},{9,8},{10,11... | collective-permute-start | bytes 589832 | tf_op jit(solution)/shard_map/ppermute | solution.py:59
  31.2 1.7 %collective-permute-start.11 = (bf16[16,6144]{1,0:T(8,128)(2,1)S(1)}, bf16[16,6144]{1,0:T(8,128)(2,1)S(1)}, u32[]{:S(2)}, u32[]{:S(2)}) collective-permute-start(bf16[16,6144]{1,0:T(8,128)(2,1)S(1)} %collective-permute-done.8), channel_id=1, source_target_pairs={{0,1},{1,0},{2,3},{3,2},{4,5},{5,4},{6,7},{7,6},{8,9},{9,8},{10,11... | collective-permute-start | bytes 589832 | tf_op jit(solution)/shard_map/ppermute | solution.py:59
  43.8 2.4 %collective-permute-start.13 = (f16[64,6144]{1,0:T(8,128)(2,1)S(1)}, f16[64,6144]{1,0:T(8,128)(2,1)S(1)}, u32[]{:S(2)}, u32[]{:S(2)}) collective-permute-start(f16[64,6144]{1,0:T(8,128)(2,1)S(1)} %convert_element_type.56), channel_id=1, source_target_pairs={{0,1},{1,0},{2,3},{3,2},{4,5},{5,4},{6,7},{7,6},{8,9},{9,8},{10,11... | collective-permute-start | bytes 2359304 | tf_op jit(solution)/shard_map/ppermute | solution.py:59
  44.2 4.4 %collective-permute-start.12 = (f16[64,6144]{1,0:T(8,128)(2,1)S(1)}, f16[64,6144]{1,0:T(8,128)(2,1)S(1)}, u32[]{:S(2)}, u32[]{:S(2)}) collective-permute-start(f16[64,6144]{1,0:T(8,128)(2,1)S(1)} %convert_element_type.54), channel_id=1, source_target_pairs={{0,1},{1,0},{2,3},{3,2},{4,5},{5,4},{6,7},{7,6},{8,9},{9,8},{10,11... | collective-permute-start | bytes 2359304 | tf_op jit(solution)/shard_map/ppermute | solution.py:59
  46.5 7.8 %collective-permute-start.14 = (f16[16,6144]{1,0:T(8,128)(2,1)S(1)}, f16[16,6144]{1,0:T(8,128)(2,1)S(1)}, u32[]{:S(2)}, u32[]{:S(2)}) collective-permute-start(f16[16,6144]{1,0:T(8,128)(2,1)S(1)} %get-tuple-element.67), channel_id=1, source_target_pairs={{0,4},{1,5},{2,6},{3,7},{4,0},{5,1},{6,2},{7,3},{8,12},{9,13},{10,... | collective-permute-start | bytes 589832 | tf_op jit(solution)/shard_map/ppermute | solution.py:59
  47.1 11.4 %collective-permute-start.19 = (f16[16,6144]{1,0:T(8,128)(2,1)S(1)}, f16[16,6144]{1,0:T(8,128)(2,1)S(1)}, u32[]{:S(2)}, u32[]{:S(2)}) collective-permute-start(f16[16,6144]{1,0:T(8,128)(2,1)S(1)} %get-tuple-element.68), channel_id=1, source_target_pairs={{0,4},{1,5},{2,6},{3,7},{4,0},{5,1},{6,2},{7,3},{8,12},{9,13},{10,... | collective-permute-start | bytes 589832 | tf_op jit(solution)/shard_map/ppermute | solution.py:59
  48.9 6.5 %collective-permute-start.17 = (f16[16,6144]{1,0:T(8,128)(2,1)S(1)}, f16[16,6144]{1,0:T(8,128)(2,1)S(1)}, u32[]{:S(2)}, u32[]{:S(2)}) collective-permute-start(f16[16,6144]{1,0:T(8,128)(2,1)S(1)} %get-tuple-element.66), channel_id=1, source_target_pairs={{0,2},{1,3},{2,0},{3,1},{4,6},{5,7},{6,4},{7,5},{8,10},{9,11},{10,... | collective-permute-start | bytes 589832 | tf_op jit(solution)/shard_map/ppermute | solution.py:59
  54.3 5.7 %collective-permute-start.15 = (f16[16,6144]{1,0:T(8,128)(2,1)S(1)}, f16[16,6144]{1,0:T(8,128)(2,1)S(1)}, u32[]{:S(2)}, u32[]{:S(2)}) collective-permute-start(f16[16,6144]{1,0:T(8,128)(2,1)S(1)} %fusion.3), channel_id=1, source_target_pairs={{0,2},{1,3},{2,0},{3,1},{4,6},{5,7},{6,4},{7,5},{8,10},{9,11},{10,... | collective-permute-start | bytes 589832 | tf_op jit(solution)/shard_map/ppermute | solution.py:59
  55.5 12.4 %copy-start = (bf16[16,6144]{1,0:T(8,128)(2,1)S(1)}, bf16[16,6144]{1,0:T(8,128)(2,1)}, u32[]{:S(2)}) copy-start(bf16[16,6144]{1,0:T(8,128)(2,1)} %adjoint_ref.1) | copy-start | bytes 589828
  55.5 12.4 %copy-start.1 = (f32[6144]{0:T(1024)S(1)}, f32[6144]{0:T(1024)}, u32[]{:S(2)}) copy-start(f32[6144]{0:T(1024)} %param.11) | copy-start | bytes 73732
  55.5 6.9 %collective-permute-start.18 = (f16[16,6144]{1,0:T(8,128)(2,1)S(1)}, f16[16,6144]{1,0:T(8,128)(2,1)S(1)}, u32[]{:S(2)}, u32[]{:S(2)}) collective-permute-start(f16[16,6144]{1,0:T(8,128)(2,1)S(1)} %fusion.2), channel_id=1, source_target_pairs={{0,4},{1,5},{2,6},{3,7},{4,0},{5,1},{6,2},{7,3},{8,12},{9,13},{10,... | collective-permute-start | bytes 589832 | tf_op jit(solution)/shard_map/ppermute | solution.py:59
  60.2 7.6 %collective-permute-start.20 = (f16[16,6144]{1,0:T(8,128)(2,1)S(1)}, f16[16,6144]{1,0:T(8,128)(2,1)S(1)}, u32[]{:S(2)}, u32[]{:S(2)}) collective-permute-start(f16[16,6144]{1,0:T(8,128)(2,1)S(1)} %fusion.1), channel_id=1, source_target_pairs={{0,12},{1,13},{2,14},{3,15},{4,8},{5,9},{6,10},{7,11},{8,4},{9,5},... | collective-permute-start | bytes 589832 | tf_op jit(solution)/shard_map/ppermute | solution.py:59
  61.8 6.0 %collective-permute-start.16 = (f16[16,6144]{1,0:T(8,128)(2,1)S(1)}, f16[16,6144]{1,0:T(8,128)(2,1)S(1)}, u32[]{:S(2)}, u32[]{:S(2)}) collective-permute-start(f16[16,6144]{1,0:T(8,128)(2,1)S(1)} %get-tuple-element.57), channel_id=1, source_target_pairs={{0,2},{1,3},{2,0},{3,1},{4,6},{5,7},{6,4},{7,5},{8,10},{9,11},{10,... | collective-permute-start | bytes 589832 | tf_op jit(solution)/shard_map/ppermute | solution.py:59
